TPU v7x, 128 devices: a whole 4x4x4 slice. The times are simulated.
128 devices in a mesh: dom: 128 (over y, z, x, core).
Axes of the slice: x: 4, y: 4, z: 4, core: 2. Of those that a mesh axis runs over, the one named last changes fastest.
Arguments:
- primal: float32 [81, 262144], P(None, 'dom'), may hold values from -6 to 6
- dual: float32 [81, 262144], P(None, 'dom'), may hold values from -6 to 6
- load: float32 [81, 262144], P(None, 'dom'), may hold values from -6 to 6
- cell_size: float32 [262144], P('dom'), may hold values from 0.05 to 1.5
- cell_count: int32 [128], replicated, may hold values from 256 to 2048, as said below
- ghost_send: int32 [128, 8, 256], P('dom'), may hold values from 0 to 2047, as said below
- face_cell: int32 [786432], P('dom'), may hold values from 0 to 2047, as said below
- face_other: int32 [786432], P('dom'), may hold values from 0 to 4095, as said below
- face_dir: int32 [786432], P('dom'), may hold values from 0 to 5
- hanging: int32 [786432], P('dom'), may hold values 0 or 1
- stiffness: float32 [81, 81], replicated, may hold values from -0.625 to 0.625
- recon: float32 [648, 648], replicated, may hold values from -0.25 to 0.25
- traction: float32 [162, 81], replicated, may hold values from -0.15625 to 0.15625
- trace: float32 [162, 81], replicated, may hold values from -0.625 to 0.625
Outputs:
- indicator: float32 [262144], P('dom')
- share: float32 [262144], P('dom')
Inputs may be any that keep to these rules, and one draw needn't show every extreme that they name: `cell_count`: the sum over partitions is a multiple of 8. ghost_send[s, k] holds 256 distinct live slots of partition s. `face_cell`: a live slot of the face's partition. `face_other`: below 2048: a live slot of the face's partition other than face_cell; otherwise a ghost entry whose source partition r - o_k lies in 0 to 127.
All inputs are finite; a program needn't handle non-finite values. No bound on the sum of `hanging` on one device may be relied on, other than what follows from the above.
Results may differ from a plain program's by a relative error of at most 0.0003.
Values sent between devices are 32-bit elements; how exact they have to be, the bound alone decides.
A program may use at most 192 MiB of HBM per device.

v0:
```python
import jax
import jax.numpy as jnp
from jax import lax
from jax.sharding import PartitionSpec as P

FACE_DOF = 27
DIRS = 6
CHILD = 8


precise = lax.Precision.HIGHEST


def from_behind(shard, axis, by):
    size = lax.axis_size(axis)
    pairs = [(i, i + by) for i in range(size) if 0 <= i + by < size]
    return lax.ppermute(shard, axis, pairs)


def rebuild(columns, recon):
    node_rows = columns.shape[0]
    blocks = columns.shape[1] // CHILD
    family = (
        columns.reshape(node_rows, blocks, CHILD)
        .transpose(2, 0, 1)
        .reshape(CHILD * node_rows, blocks)
    )
    rebuilt = jnp.dot(recon, family, precision=precise, preferred_element_type=jnp.float32)
    return (
        rebuilt.reshape(CHILD, node_rows, blocks)
        .transpose(1, 2, 0)
        .reshape(node_rows, blocks * CHILD)
    )


def pick_direction(all_rows, direction):
    width_cols = all_rows.shape[1]
    dir_table = all_rows.reshape(DIRS, FACE_DOF, width_cols)
    onehot = (direction[None, :] == jnp.arange(DIRS, dtype=jnp.int32)[:, None]).astype(jnp.float32)
    return jnp.sum(dir_table * onehot[:, None, :], axis=0)


def per_device(
    primal,
    dual,
    load,
    cell_size,
    cell_count,
    ghost_send,
    face_cell,
    face_other,
    face_dir,
    hanging,
    stiffness,
    recon,
    traction,
    trace,
):
    rank_total = lax.axis_size("dom")
    rank_here = lax.axis_index("dom")
    node_rows, slot_count = primal.shape
    list_count = ghost_send.shape[1]
    ghost_len = ghost_send.shape[2]
    rank_order = jnp.arange(rank_total, dtype=jnp.int32)
    live_count = jnp.sum(jnp.where(rank_order == rank_here, cell_count, 0))
    live_start = jnp.sum(jnp.where(rank_order < rank_here, cell_count, 0))
    live_total = jnp.sum(cell_count)
    head_cells = (CHILD - live_start % CHILD) % CHILD
    tail_cells = (live_count - head_cells) % CHILD
    first_block = dual[:, :CHILD]
    next_first = from_behind(first_block, "dom", -1)
    spare = jnp.zeros((node_rows, CHILD), jnp.float32)
    shifted = lax.dynamic_slice_in_dim(jnp.concatenate([dual, spare], 1), head_cells, slot_count, 1)
    shifted = jnp.concatenate([shifted, spare], 1)
    shifted = lax.dynamic_update_slice_in_dim(shifted, next_first, live_count - head_cells, 1)
    rebuilt = rebuild(shifted, recon)
    outgoing_family = lax.dynamic_slice_in_dim(
        rebuilt, live_count - head_cells - tail_cells, CHILD, 1
    )
    head_family = from_behind(outgoing_family, "dom", 1)
    joined = jnp.concatenate([head_family, rebuilt], 1)
    weight = lax.dynamic_slice_in_dim(joined, CHILD - head_cells, slot_count, 1)
    live_mask = jnp.arange(slot_count, dtype=jnp.int32) < live_count
    weight = jnp.where(live_mask[None, :], weight, jnp.float32(0.0))
    residual = load - jnp.dot(
        stiffness, primal, precision=precise, preferred_element_type=jnp.float32
    )
    cell_term = cell_size * jnp.sum(residual * weight, axis=0)
    cell_rows = jnp.concatenate([primal, weight], 0)
    send_lists = ghost_send[0].reshape(-1)
    outgoing = jnp.moveaxis(
        cell_rows[:, send_lists].reshape(2 * node_rows, list_count, ghost_len), 1, 0
    )
    shifts = [(1 << which // 2) * (1 - 2 * (which % 2)) for which in range(list_count)]
    pieces = [from_behind(outgoing[which], "dom", shifts[which]) for which in range(list_count)]
    incoming = jnp.stack(pieces, 0)
    ghost_rows_all = jnp.moveaxis(incoming, 0, 1).reshape(2 * node_rows, list_count * ghost_len)
    extended = jnp.concatenate([cell_rows, ghost_rows_all], 1)
    side_a = extended[:, face_cell]
    side_b = extended[:, face_other]
    dir_b = face_dir + 1 - 2 * (face_dir % 2)
    face_total = face_cell.shape[0]
    live_face = jnp.arange(face_total, dtype=jnp.int32) < 3 * live_count
    face_area = jnp.where(live_face, 1.0 - 0.75 * hanging.astype(jnp.float32), jnp.float32(0.0))
    trac_a = pick_direction(
        jnp.dot(
            traction, side_a[:node_rows], precision=precise, preferred_element_type=jnp.float32
        ),
        face_dir,
    )
    trac_b = pick_direction(
        jnp.dot(
            traction, side_b[:node_rows], precision=precise, preferred_element_type=jnp.float32
        ),
        dir_b,
    )
    trace_a = pick_direction(
        jnp.dot(trace, side_a[node_rows:], precision=precise, preferred_element_type=jnp.float32),
        face_dir,
    )
    trace_b = pick_direction(
        jnp.dot(trace, side_b[node_rows:], precision=precise, preferred_element_type=jnp.float32),
        dir_b,
    )
    face_jump = trac_a + trac_b
    term_a = 0.5 * face_area * jnp.sum(face_jump * trace_a, axis=0)
    term_b = 0.5 * face_area * jnp.sum(face_jump * trace_b, axis=0)
    face_sums = (
        jnp.zeros((extended.shape[1],), jnp.float32)
        .at[face_cell]
        .add(term_a)
        .at[face_other]
        .add(term_b)
    )
    indicator = cell_term + face_sums[:slot_count]
    partial_terms = face_sums[slot_count:].reshape(list_count, ghost_len)
    returned = jnp.stack(
        [from_behind(partial_terms[which], "dom", -shifts[which]) for which in range(list_count)], 0
    )
    indicator = indicator + jnp.zeros((slot_count,), jnp.float32).at[send_lists].add(
        returned.reshape(-1)
    )
    indicator = jnp.where(live_mask, indicator, jnp.float32(0.0))
    abs_sum = lax.psum(jnp.sum(jnp.abs(indicator)), "dom")
    mean_abs = abs_sum / live_total.astype(jnp.float32)
    share = jnp.abs(indicator) / (mean_abs + 1e-06)
    return (indicator, share)


def solution(mesh):
    in_specs = (
        P(None, "dom"),
        P(None, "dom"),
        P(None, "dom"),
        P("dom"),
        P(),
        P("dom", None, None),
        P("dom"),
        P("dom"),
        P("dom"),
        P("dom"),
        P(),
        P(),
        P(),
        P(),
    )
    out_specs = (P("dom"), P("dom"))
    return jax.shard_map(
        per_device, mesh=mesh, in_specs=in_specs, out_specs=out_specs, check_vma=False
    )
```

profile of v0, /device:TPU:0, one launch (start us, length us, event | category | flops | bytes accessed | tf_op | source)
XLA Modules:
  0.0 410.0 jit_solution(10358556215199448350)
XLA Ops:
  17.4 3.4 convolution_bitcast_fusion.4
  21.8 3.0 collective-permute-start.1
  28.3 2.8 copy.45
  31.0 10.1 %gather_fusion = f32[2048,162]{1,0:T(8,128)} fusion(f32[162,2048]{0,1:T(8,128)} %copy.45, s32[2048]{0:T(1024)S(1)} %broadcast_clamp_fusion.2), kind=kCustom, calls=%fused_computation | custom fusion | bytes 2662400 | tf_op jit(solution)/shard_map/gather | solution.py:92
  41.2 2.8 copy.46
  45.5 8.7 %collective-permute-start.8 = (f32[162,256]{1,0:T(8,128)S(1)}, f32[162,256]{1,0:T(8,128)S(1)}, u32[]{:S(2)}, u32[]{:S(2)}) collective-permute-start(f32[162,256]{1,0:T(8,128)S(1)} %get-tuple-element.14), channel_id=1, source_target_pairs={{0,8},{1,9},{2,10},{3,11},{4,12},{5,13},{6,14},{7,15},{8,16},{9,17... | collective-permute-start | bytes 497672 | tf_op jit(solution)/shard_map/ppermute | solution.py:17
  55.5 6.1 %collective-permute-start.6 = (f32[162,256]{1,0:T(8,128)S(1)}, f32[162,256]{1,0:T(8,128)S(1)}, u32[]{:S(2)}, u32[]{:S(2)}) collective-permute-start(f32[162,256]{1,0:T(8,128)S(1)} %get-tuple-element.16), channel_id=1, source_target_pairs={{0,4},{1,5},{2,6},{3,7},{4,8},{5,9},{6,10},{7,11},{8,12},{9,13},{1... | collective-permute-start | bytes 497672 | tf_op jit(solution)/shard_map/ppermute | solution.py:17
  64.2 4.6 %collective-permute-start.4 = (f32[162,256]{1,0:T(8,128)S(1)}, f32[162,256]{1,0:T(8,128)S(1)}, u32[]{:S(2)}, u32[]{:S(2)}) collective-permute-start(f32[162,256]{1,0:T(8,128)S(1)} %get-tuple-element.18), channel_id=1, source_target_pairs={{0,2},{1,3},{2,4},{3,5},{4,6},{5,7},{6,8},{7,9},{8,10},{9,11},{10,... | collective-permute-start | bytes 497672 | tf_op jit(solution)/shard_map/ppermute | solution.py:17
  70.1 3.0 collective-permute-start.2
  74.6 3.5 stack.62
  80.1 1.8 pad_maximum_fusion
  81.9 5.0 %copy.54 = f32[162,4096]{0,1:T(8,128)} copy(f32[162,4096]{1,0:T(8,128)} %pad_maximum_fusion) | data formatting | bytes 5308416 | tf_op jit(solution)/shard_map/concatenate | solution.py:98
  86.8 25.9 %gather_fusion.2 = f32[6144,162]{1,0:T(8,128)} fusion(f32[162,4096]{0,1:T(8,128)} %copy.54, s32[6144]{0:T(1024)S(1)} %get-tuple-element.24), kind=kCustom, calls=%fused_computation.2 | custom fusion | bytes 7987200 | tf_op jit(solution)/shard_map/gather | solution.py:100
  112.8 25.9 %gather_fusion.1 = f32[6144,162]{1,0:T(8,128)} fusion(f32[162,4096]{0,1:T(8,128)} %copy.54, s32[6144]{0:T(1024)S(1)} %get-tuple-element.25), kind=kCustom, calls=%fused_computation.1 | custom fusion | bytes 7987200 | tf_op jit(solution)/shard_map/gather | solution.py:99
  138.7 7.7 %convolution_bitcast_fusion.3 = f32[162,6144]{1,0:T(8,128)} fusion(f32[162,81]{1,0:T(8,128)S(1)} %copy-done.8, f32[162,6144]{0,1:T(8,128)} %bitcast.77), kind=kOutput, calls=%fused_computation.9 | convolution fusion | flops 967458816 | bytes 7179528 | tf_op jit(solution)/shard_map/dot_general | solution.py:106
  146.4 5.5 %convolution_bitcast_fusion.1 = f32[162,6144]{1,0:T(8,128)} fusion(f32[162,81]{1,0:T(8,128)S(1)} %copy-done.9, f32[162,6144]{0,1:T(8,128)S(1)} %bitcast.78), kind=kOutput, calls=%fused_computation.7 | convolution fusion | flops 967458816 | bytes 7213056 | tf_op jit(solution)/shard_map/dot_general | solution.py:118
  151.9 5.3 %convolution_bitcast_fusion.2 = f32[162,6144]{1,0:T(8,128)} fusion(f32[162,81]{1,0:T(8,128)S(1)} %copy-done.8, f32[162,6144]{0,1:T(8,128)S(1)} %bitcast.75), kind=kOutput, calls=%fused_computation.8 | convolution fusion | flops 967458816 | bytes 7213056 | tf_op jit(solution)/shard_map/dot_general | solution.py:112
  157.2 5.6 %convolution_bitcast_fusion = f32[162,6144]{1,0:T(8,128)} fusion(f32[162,81]{1,0:T(8,128)S(1)} %copy-done.9, f32[162,6144]{0,1:T(8,128)S(1)} %bitcast.76), kind=kOutput, calls=%fused_computation.6 | convolution fusion | flops 967458816 | bytes 7213056 | tf_op jit(solution)/shard_map/dot_general | solution.py:122
  162.8 4.8 %reshape.130 = f32[6,27,6144]{2,1,0:T(8,128)} reshape(f32[162,6144]{1,0:T(8,128)} %convolution_bitcast_fusion.1) | data formatting | bytes 7962624 | tf_op jit(solution)/shard_map/reshape | solution.py:38
  167.6 4.9 %reshape.128 = f32[6,27,6144]{2,1,0:T(8,128)} reshape(f32[162,6144]{1,0:T(8,128)} %convolution_bitcast_fusion.3) | data formatting | bytes 7962624 | tf_op jit(solution)/shard_map/reshape | solution.py:38
  172.5 4.8 %reshape.131 = f32[6,27,6144]{2,1,0:T(8,128)} reshape(f32[162,6144]{1,0:T(8,128)} %convolution_bitcast_fusion) | data formatting | bytes 7962624 | tf_op jit(solution)/shard_map/reshape | solution.py:38
  177.3 4.9 %reshape.129 = f32[6,27,6144]{2,1,0:T(8,128)} reshape(f32[162,6144]{1,0:T(8,128)} %convolution_bitcast_fusion.2) | data formatting | bytes 7962624 | tf_op jit(solution)/shard_map/reshape | solution.py:38
  182.2 7.9 %multiply_reduce_fusion = (f32[27,6144]{1,0:T(8,128)S(1)}, f32[27,6144]{1,0:T(8,128)S(1)}, f32[27,6144]{1,0:T(8,128)S(1)}, f32[27,6144]{1,0:T(8,128)S(1)}) fusion(f32[6,27,6144]{2,1,0:T(8,128)} %reshape.131, f32[6,6144]{1,0:T(8,128)S(1)} %copy-done.6, f32[6,27,6144]{2,1,0:T(8,128)} %reshape.129, f32[6,27,6144]{2,1,0:T(8,128)} %reshape.130, ...), kind=kLoop, calls=%fused_computation.10 | loop fusion | flops 7299072 | bytes 18874368 | tf_op jit(solution)/shard_map/reduce_sum | solution.py:40
  190.5 42.9 %scatter_custom_fusion = f32[4096]{0:T(1024)S(1)} fusion(s32[6144]{0:T(1024)S(1)} %get-tuple-element.26, f32[6144]{0:T(1024)S(1)} %get-tuple-element.22, f32[]{:T(128)} %constant.54.clone.1), kind=kCustom, calls=%fused_computation.60 | custom fusion | flops 6144 | bytes 16388 | tf_op jit(solution)/shard_map/scatter-add | solution.py:131
  233.4 35.0 %scatter_fusion = f32[4096]{0:T(1024)S(1)} fusion(f32[4096]{0:T(1024)S(1)} %scatter_custom_fusion, s32[6144]{0:T(1024)S(1)} %get-tuple-element.23, f32[6144]{0:T(1024)S(1)} %get-tuple-element.21), kind=kCustom, calls=%fused_computation.4 | custom fusion | flops 6144 | bytes 98304 | tf_op jit(solution)/shard_map/scatter-add | solution.py:133
  268.5 9.3 %collective-permute-start.17 = (f32[256]{0:T(256)S(1)}, f32[256]{0:T(256)S(1)}, u32[]{:S(2)}, u32[]{:S(2)}) collective-permute-start(f32[256]{0:T(256)S(1)} %get-tuple-element.27), channel_id=1, source_target_pairs={{0,8},{1,9},{2,10},{3,11},{4,12},{5,13},{6,14},{7,15},{8,16},{9,17... | collective-permute-start | bytes 3080 | tf_op jit(solution)/shard_map/ppermute | solution.py:17
  282.4 2.7 collective-permute-start.13
  286.5 2.4 collective-permute-start.11
  291.3 3.8 collective-permute-done.12
  295.1 3.1 collective-permute-done.10
  298.2 14.7 %scatter_fusion.1 = f32[2048]{0:T(1024)S(1)} fusion(f32[2048]{0:T(1024)S(1)} %slice_add_fusion, s32[2048]{0:T(1024)S(1)} %bitcast.94, f32[2048]{0:T(1024)S(1)} %bitcast.95), kind=kCustom, calls=%fused_computation.5 | custom fusion | flops 2048 | bytes 32768 | tf_op jit(solution)/shard_map/scatter-add | solution.py:140
  314.2 94.5 %psum.7 = f32[]{:T(128)} all-reduce(f32[]{:T(128)} %get-tuple-element.11), channel_id=1, replica_groups=mesh['dom'=128] {'dom'}, use_global_device_ids=true, to_apply=%region_13.14 | all-reduce | flops 1 | bytes 8 | tf_op jit(solution)/shard_map/psum | solution.py:144
  (99 shorter events, 37.6 us)
Async XLA Ops:
  0.6 16.7 %copy-start = (f32[648,648]{1,0:T(8,128)S(1)}, f32[648,648]{1,0:T(8,128)}, u32[]{:S(2)}) copy-start(f32[648,648]{1,0:T(8,128)} %param.25) | copy-start | bytes 5038852
  1.6 11.4 %collective-permute-start = (f32[81,8]{1,0:T(8,128)S(1)}, f32[81,8]{1,0:T(8,128)S(1)}, u32[]{:S(2)}, u32[]{:S(2)}) collective-permute-start(f32[81,8]{1,0:T(8,128)S(1)} %slice.83), channel_id=1, source_target_pairs={{1,0},{2,1},{3,2},{4,3},{5,4},{6,5},{7,6},{8,7},{9,8},{10,9},{11,1... | collective-permute-start | bytes 7784 | tf_op jit(solution)/shard_map/ppermute | solution.py:17
  17.3 9.7 %copy-start.4 = (f32[81,2048]{1,0:T(8,128)S(1)}, f32[81,2048]{1,0:T(8,128)}, u32[]{:S(2)}) copy-start(f32[81,2048]{1,0:T(8,128)} %param.14) | copy-start | bytes 1990660
  21.8 5.0 %collective-permute-start.1 = (f32[81,8]{1,0:T(8,128)S(1)}, f32[81,8]{1,0:T(8,128)S(1)}, u32[]{:S(2)}, u32[]{:S(2)}) collective-permute-start(f32[81,8]{1,0:T(8,128)S(1)} %constant_dynamic-slice_fusion), channel_id=1, source_target_pairs={{0,1},{1,2},{2,3},{3,4},{4,5},{5,6},{6,7},{7,8},{8,9},{9,10},{10,1... | collective-permute-start | bytes 7784 | tf_op jit(solution)/shard_map/ppermute | solution.py:17
  41.2 20.4 %copy-start.12 = (s32[6144]{0:T(1024)S(1)}, s32[6144]{0:T(1024)}, u32[]{:S(2)}) copy-start(s32[6144]{0:T(1024)} %param.20) | copy-start | bytes 73732
  41.2 32.0 %copy-start.13 = (s32[6144]{0:T(1024)S(1)}, s32[6144]{0:T(1024)}, u32[]{:S(2)}) copy-start(s32[6144]{0:T(1024)} %param.21) | copy-start | bytes 73732
  45.5 18.8 %collective-permute-start.8 = (f32[162,256]{1,0:T(8,128)S(1)}, f32[162,256]{1,0:T(8,128)S(1)}, u32[]{:S(2)}, u32[]{:S(2)}) collective-permute-start(f32[162,256]{1,0:T(8,128)S(1)} %get-tuple-element.14), channel_id=1, source_target_pairs={{0,8},{1,9},{2,10},{3,11},{4,12},{5,13},{6,14},{7,15},{8,16},{9,17... | collective-permute-start | bytes 497672 | tf_op jit(solution)/shard_map/ppermute | solution.py:17
  54.2 14.6 %collective-permute-start.7 = (f32[162,256]{1,0:T(8,128)S(1)}, f32[162,256]{1,0:T(8,128)S(1)}, u32[]{:S(2)}, u32[]{:S(2)}) collective-permute-start(f32[162,256]{1,0:T(8,128)S(1)} %get-tuple-element.15), channel_id=1, source_target_pairs={{4,0},{5,1},{6,2},{7,3},{8,4},{9,5},{10,6},{11,7},{12,8},{13,9},{1... | collective-permute-start | bytes 497672 | tf_op jit(solution)/shard_map/ppermute | solution.py:17
  55.5 14.6 %collective-permute-start.6 = (f32[162,256]{1,0:T(8,128)S(1)}, f32[162,256]{1,0:T(8,128)S(1)}, u32[]{:S(2)}, u32[]{:S(2)}) collective-permute-start(f32[162,256]{1,0:T(8,128)S(1)} %get-tuple-element.16), channel_id=1, source_target_pairs={{0,4},{1,5},{2,6},{3,7},{4,8},{5,9},{6,10},{7,11},{8,12},{9,13},{1... | collective-permute-start | bytes 497672 | tf_op jit(solution)/shard_map/ppermute | solution.py:17
  61.6 12.9 %collective-permute-start.9 = (f32[162,256]{1,0:T(8,128)S(1)}, f32[162,256]{1,0:T(8,128)S(1)}, u32[]{:S(2)}, u32[]{:S(2)}) collective-permute-start(f32[162,256]{1,0:T(8,128)S(1)} %get-tuple-element.13), channel_id=1, source_target_pairs={{8,0},{9,1},{10,2},{11,3},{12,4},{13,5},{14,6},{15,7},{16,8},{17,9... | collective-permute-start | bytes 497672 | tf_op jit(solution)/shard_map/ppermute | solution.py:17
  62.9 10.8 %collective-permute-start.5 = (f32[162,256]{1,0:T(8,128)S(1)}, f32[162,256]{1,0:T(8,128)S(1)}, u32[]{:S(2)}, u32[]{:S(2)}) collective-permute-start(f32[162,256]{1,0:T(8,128)S(1)} %get-tuple-element.17), channel_id=1, source_target_pairs={{2,0},{3,1},{4,2},{5,3},{6,4},{7,5},{8,6},{9,7},{10,8},{11,9},{12,... | collective-permute-start | bytes 497672 | tf_op jit(solution)/shard_map/ppermute | solution.py:17
  64.2 9.7 %collective-permute-start.4 = (f32[162,256]{1,0:T(8,128)S(1)}, f32[162,256]{1,0:T(8,128)S(1)}, u32[]{:S(2)}, u32[]{:S(2)}) collective-permute-start(f32[162,256]{1,0:T(8,128)S(1)} %get-tuple-element.18), channel_id=1, source_target_pairs={{0,2},{1,3},{2,4},{3,5},{4,6},{5,7},{6,8},{7,9},{8,10},{9,11},{10,... | collective-permute-start | bytes 497672 | tf_op jit(solution)/shard_map/ppermute | solution.py:17
  68.8 5.3 %collective-permute-start.3 = (f32[162,256]{1,0:T(8,128)S(1)}, f32[162,256]{1,0:T(8,128)S(1)}, u32[]{:S(2)}, u32[]{:S(2)}) collective-permute-start(f32[162,256]{1,0:T(8,128)S(1)} %get-tuple-element.19), channel_id=1, source_target_pairs={{1,0},{2,1},{3,2},{4,3},{5,4},{6,5},{7,6},{8,7},{9,8},{10,9},{11,1... | collective-permute-start | bytes 497672 | tf_op jit(solution)/shard_map/ppermute | solution.py:17
  70.1 4.2 %collective-permute-start.2 = (f32[162,256]{1,0:T(8,128)S(1)}, f32[162,256]{1,0:T(8,128)S(1)}, u32[]{:S(2)}, u32[]{:S(2)}) collective-permute-start(f32[162,256]{1,0:T(8,128)S(1)} %get-tuple-element.20), channel_id=1, source_target_pairs={{0,1},{1,2},{2,3},{3,4},{4,5},{5,6},{6,7},{7,8},{8,9},{9,10},{10,1... | collective-permute-start | bytes 497672 | tf_op jit(solution)/shard_map/ppermute | solution.py:17
  112.8 25.9 %copy-start.8 = (f32[162,81]{1,0:T(8,128)S(1)}, f32[162,81]{1,0:T(8,128)}, u32[]{:S(2)}) copy-start(f32[162,81]{1,0:T(8,128)} %param.26) | copy-start | bytes 157468
  138.7 7.7 %copy-start.3 = (f32[6144,162]{1,0:T(8,128)S(1)}, f32[6144,162]{1,0:T(8,128)}, u32[]{:S(2)}) copy-start(f32[6144,162]{1,0:T(8,128)} %gather_fusion.1) | copy-start | bytes 11943940
  138.7 7.7 %copy-start.9 = (f32[162,81]{1,0:T(8,128)S(1)}, f32[162,81]{1,0:T(8,128)}, u32[]{:S(2)}) copy-start(f32[162,81]{1,0:T(8,128)} %param.27) | copy-start | bytes 157468
  146.4 5.5 %copy-start.2 = (f32[6144,162]{1,0:T(8,128)S(1)}, f32[6144,162]{1,0:T(8,128)}, u32[]{:S(2)}) copy-start(f32[6144,162]{1,0:T(8,128)} %gather_fusion.2) | copy-start | bytes 11943940
  182.2 8.2 %copy-start.14 = (s32[6144]{0:T(1024)S(1)}, s32[6144]{0:T(1024)}, u32[]{:S(2)}) copy-start(s32[6144]{0:T(1024)} %param.23) | copy-start | bytes 73732
  233.4 47.0 %copy-start.7 = (f32[81,2048]{1,0:T(8,128)S(1)}, f32[81,2048]{1,0:T(8,128)}, u32[]{:S(2)}) copy-start(f32[81,2048]{1,0:T(8,128)} %param.16) | copy-start | bytes 1990660
  233.4 47.0 %copy-start.10 = (f32[81,81]{1,0:T(8,128)S(1)}, f32[81,81]{1,0:T(8,128)}, u32[]{:S(2)}) copy-start(f32[81,81]{1,0:T(8,128)} %param.24) | copy-start | bytes 78736
  233.4 56.8 %copy-start.15 = (f32[2048]{0:T(1024)S(1)}, f32[2048]{0:T(1024)}, u32[]{:S(2)}) copy-start(f32[2048]{0:T(1024)} %param.17) | copy-start | bytes 24580
  268.5 16.7 %collective-permute-start.17 = (f32[256]{0:T(256)S(1)}, f32[256]{0:T(256)S(1)}, u32[]{:S(2)}, u32[]{:S(2)}) collective-permute-start(f32[256]{0:T(256)S(1)} %get-tuple-element.27), channel_id=1, source_target_pairs={{0,8},{1,9},{2,10},{3,11},{4,12},{5,13},{6,14},{7,15},{8,16},{9,17... | collective-permute-start | bytes 3080 | tf_op jit(solution)/shard_map/ppermute | solution.py:17
  277.8 8.7 %collective-permute-start.16 = (f32[256]{0:T(256)S(1)}, f32[256]{0:T(256)S(1)}, u32[]{:S(2)}, u32[]{:S(2)}) collective-permute-start(f32[256]{0:T(256)S(1)} %get-tuple-element.28), channel_id=1, source_target_pairs={{8,0},{9,1},{10,2},{11,3},{12,4},{13,5},{14,6},{15,7},{16,8},{17,9... | collective-permute-start | bytes 3080 | tf_op jit(solution)/shard_map/ppermute | solution.py:17
  279.1 9.9 %collective-permute-start.15 = (f32[256]{0:T(256)S(1)}, f32[256]{0:T(256)S(1)}, u32[]{:S(2)}, u32[]{:S(2)}) collective-permute-start(f32[256]{0:T(256)S(1)} %get-tuple-element.29), channel_id=1, source_target_pairs={{0,4},{1,5},{2,6},{3,7},{4,8},{5,9},{6,10},{7,11},{8,12},{9,13},{1... | collective-permute-start | bytes 3080 | tf_op jit(solution)/shard_map/ppermute | solution.py:17
  281.1 10.2 %collective-permute-start.14 = (f32[256]{0:T(256)S(1)}, f32[256]{0:T(256)S(1)}, u32[]{:S(2)}, u32[]{:S(2)}) collective-permute-start(f32[256]{0:T(256)S(1)} %get-tuple-element.30), channel_id=1, source_target_pairs={{4,0},{5,1},{6,2},{7,3},{8,4},{9,5},{10,6},{11,7},{12,8},{13,9},{1... | collective-permute-start | bytes 3080 | tf_op jit(solution)/shard_map/ppermute | solution.py:17
  282.4 8.9 %collective-permute-start.13 = (f32[256]{0:T(256)S(1)}, f32[256]{0:T(256)S(1)}, u32[]{:S(2)}, u32[]{:S(2)}) collective-permute-start(f32[256]{0:T(256)S(1)} %get-tuple-element.31), channel_id=1, source_target_pairs={{0,2},{1,3},{2,4},{3,5},{4,6},{5,7},{6,8},{7,9},{8,10},{9,11},{10,... | collective-permute-start | bytes 3080 | tf_op jit(solution)/shard_map/ppermute | solution.py:17
  285.2 9.9 %collective-permute-start.12 = (f32[256]{0:T(256)S(1)}, f32[256]{0:T(256)S(1)}, u32[]{:S(2)}, u32[]{:S(2)}) collective-permute-start(f32[256]{0:T(256)S(1)} %get-tuple-element.32), channel_id=1, source_target_pairs={{2,0},{3,1},{4,2},{5,3},{6,4},{7,5},{8,6},{9,7},{10,8},{11,9},{12,... | collective-permute-start | bytes 3080 | tf_op jit(solution)/shard_map/ppermute | solution.py:17
  286.5 8.6 %collective-permute-start.11 = (f32[256]{0:T(256)S(1)}, f32[256]{0:T(256)S(1)}, u32[]{:S(2)}, u32[]{:S(2)}) collective-permute-start(f32[256]{0:T(256)S(1)} %get-tuple-element.33), channel_id=1, source_target_pairs={{0,1},{1,2},{2,3},{3,4},{4,5},{5,6},{6,7},{7,8},{8,9},{9,10},{10,1... | collective-permute-start | bytes 3080 | tf_op jit(solution)/shard_map/ppermute | solution.py:17
  288.9 9.2 %collective-permute-start.10 = (f32[256]{0:T(256)S(1)}, f32[256]{0:T(256)S(1)}, u32[]{:S(2)}, u32[]{:S(2)}) collective-permute-start(f32[256]{0:T(256)S(1)} %get-tuple-element.34), channel_id=1, source_target_pairs={{1,0},{2,1},{3,2},{4,3},{5,4},{6,5},{7,6},{8,7},{9,8},{10,9},{11,1... | collective-permute-start | bytes 3080 | tf_op jit(solution)/shard_map/ppermute | solution.py:17
  298.2 111.8 %copy-start.1 = (f32[648,648]{1,0:T(8,128)S(1)}, f32[648,648]{1,0:T(8,128)}, u32[]{:S(2)}) copy-start(f32[648,648]{1,0:T(8,128)} %param.25) | copy-start | bytes 5038852
  314.2 95.8 %copy-start.11 = (f32[2048]{0:T(1024)}, f32[2048]{0:T(1024)S(1)}, u32[]{:S(2)}) copy-start(f32[2048]{0:T(1024)S(1)} %get-tuple-element.12) | copy-start | bytes 24580
  (2 other events, 9.9 us)
where the time goes:
time: 412 us; the launch traced here: 410 us
  other arithmetic  111 us (27%)
  local copies, waits for them, and re-layouts  110 us (27%)
  blocking collectives  94.5 us (23%)
  starting transfers between devices  52.8 us (13%)
  matrix products  28.2 us (7%)
  waiting for transfers between devices  7.96 us (2%)
  between operations  5.95 us (1%)
    psum x1, blocking collectives, per_device(): abs_sum = lax.psum(jnp.sum(jnp.abs(indicator)), 'dom')  94.5 us
    scatter-add x2, other arithmetic, per_device(): face_sums = jnp.zeros((extended.shape[1],), jnp.float32).at[face_cell].ad...  77.9 us
    ppermute x18, starting transfers between devices, from_behind(): return lax.ppermute(shard, axis, pairs)  52.8 us
    gather x1, local copies, waits for them, and re-layouts, per_device(): side_a = extended[:, face_cell]  25.9 us
    gather x1, local copies, waits for them, and re-layouts, per_device(): side_b = extended[:, face_other]  25.9 us
    reshape x4, local copies, waits for them, and re-layouts, pick_direction(): dir_table = all_rows.reshape(DIRS, FACE_DOF, width_cols)  19.4 us
    scatter-add x1, other arithmetic, per_device(): jnp.zeros((slot_count,), jnp.float32).at[send_lists]  14.7 us
    gather x1, local copies, waits for them, and re-layouts, per_device(): cell_rows[:, send_lists].reshape(2 * node_rows, list_count, ghost_len)  10.1 us
  transfers between devices with their start and end apart: 18, of which 3 were waited for; matrix products, arithmetic and copies ran while one was open for 2% of the time, Pallas kernels for 0%

commit v1 on v0

v1 whole, which is shorter than its diff:
```python
import functools

import jax
import jax.numpy as jnp
from jax import lax
from jax.experimental import pallas as pl
from jax.experimental.pallas import tpu as pltpu
from jax.sharding import PartitionSpec as P

F32 = jnp.float32
BF16 = jnp.bfloat16
I32 = jnp.int32

DOF = 81
FACE_DOF = 27
CHILD = 8
CELLS = 2048
NEIGH = 8
GHOST = 256
GHOSTS = NEIGH * GHOST
SLOTS = CELLS + GHOSTS
FACES = 6144
LANES = 128
BATCH = 16
FAMILIES = 264
CHUNK = 256
CHUNKS = FACES // CHUNK
SPLIT = CHUNK // LANES


def split(x):
    high = x.astype(BF16)
    return high, (x - high.astype(F32)).astype(BF16)


def dot_nt(a, b):
    return lax.dot_general(a, b, (((1,), (1,)), ((), ())), preferred_element_type=F32)


def dot_nn(a, b):
    return lax.dot_general(a, b, (((1,), (0,)), ((), ())), preferred_element_type=F32)


def gather_rows(dst, dst_at, src, index_of, count):
    for base in range(0, count, BATCH):
        rows = [src[pl.ds(index_of(base + u), 1), :] for u in range(BATCH)]
        for u in range(BATCH):
            dst[pl.ds(dst_at + (base + u), 1), :] = rows[u]


def turned_block(src, at):
    return jnp.concatenate([src[:, pl.ds(at, 256)], jnp.zeros((LANES - DOF, 256), F32)], 0).T


def to_cell_major(dst, src, step):
    at = pl.multiple_of(step * 256, 256)
    dst[pl.ds(at, 256), :] = turned_block(src, at)


def fill_operator(operator, traction, trace):
    operator[...] = jnp.zeros(operator.shape, F32)
    for d in range(6):
        rows = slice(d * FACE_DOF, (d + 1) * FACE_DOF)
        operator[64 * d : 64 * d + FACE_DOF, 0:DOF] = traction[rows, :]
        operator[64 * d + 32 : 64 * d + 32 + FACE_DOF, LANES : LANES + DOF] = trace[rows, :]


def fill_table(table, slot, p_rows, w_rows, operator):
    o_hi, o_lo = split(operator[...])
    x_hi, x_lo = split(jnp.concatenate([p_rows[...], w_rows[...]], 1))
    out = dot_nt(x_hi, o_hi) + dot_nt(x_lo, o_hi) + dot_nt(x_hi, o_lo)
    for pair in range(3):
        table[pl.ds(pl.multiple_of(pair * SLOTS + slot, 256), 256), :] = out[:, pair * LANES : (pair + 1) * LANES]


def cell_terms(out, primal, load, w_t, cell_size, stiffness, step):
    at = pl.multiple_of(step * 256, 256)
    s_hi, s_lo = split(stiffness[...])
    p_hi, p_lo = split(primal[:, pl.ds(at, 256)])
    residual = load[:, pl.ds(at, 256)] - (dot_nn(s_hi, p_hi) + dot_nn(s_lo, p_hi) + dot_nn(s_hi, p_lo))
    weight = w_t[pl.ds(at, 256), :].T[:DOF, :]
    total = jnp.sum(residual * weight, axis=0, keepdims=True)
    for r in range(2):
        i = step * 2 + r
        out[pl.ds(i, 1), :] = cell_size[pl.ds(i, 1), :] * total[:, r * LANES : (r + 1) * LANES]


def lanes_of(ref, chunk):
    return jnp.concatenate([ref[pl.ds(chunk * SPLIT + i, 1), :] for i in range(SPLIT)], 1)


def scatter(index, value, high_count):
    width = index.shape[1]
    high = index >> 7
    low = index & 127
    chosen = lax.broadcasted_iota(I32, (high_count, width), 0) == high
    v_hi, v_lo = split(jnp.where(chosen, value, 0.0))
    onehot = jnp.where(lax.broadcasted_iota(I32, (LANES, width), 0) == low, 1.0, 0.0).astype(BF16)
    both = dot_nt(jnp.concatenate([v_hi, v_lo], 0), onehot)
    return both[:high_count] + both[high_count:]


MESH = pl.DeviceIdType.MESH
RANKS = 128
SHIFTS = [(1 << which // 2) * (1 - 2 * (which % 2)) for which in range(NEIGH)]
FIRST_LIST = 4
STAGES = ((1, 8), (8, 16))


def counts_of(counts, me):
    def body(i, carry):
        before, here = carry
        c = counts[i]
        return before + jnp.where(i < me, c, 0), here + jnp.where(i == me, c, 0)

    return lax.fori_loop(0, RANKS, body, (jnp.int32(0), jnp.int32(0)), unroll=8)


def behind(me, by):
    return lax.rem(me + (by + RANKS), RANKS)


def shift_of(k):
    e = k // 2
    power = 1 + e + e * (e - 1) // 2 + e * (e - 1) * (e - 2) // 6
    return power * (1 - 2 * (k % 2))


def in_stage(me, stride, size, step):
    place = lax.rem(me // stride, size)
    return me + (lax.rem(place + step, size) - place) * stride


def gather_list(ghosts, source, send, k):
    gather_rows(ghosts.at[k], 0, source, lambda i: send[k, i], GHOST)


def rebuild(head, live, d_t, before, after, recon_hi, recon_lo, w_t, padded, families, rebuilt, after2):
    after2[0:8, :] = after[...]
    after2[8:16, :] = after[...]
    turned = after2[pl.ds(8 - live % 8, 8), :]
    row = lax.broadcasted_iota(I32, (8, LANES), 0)
    padded[0:8, :] = before[...]

    def fill(i, carry):
        at = pl.multiple_of(i * 8, 8)
        own = d_t[pl.ds(at, 8), :]
        padded[pl.ds(at + 8, 8), :] = jnp.where(row + at < live, own, turned)
        return carry

    lax.fori_loop(0, CELLS // 8, fill, 0, unroll=8)
    padded[CELLS + 8 : CELLS + 16, :] = turned
    padded[CELLS + 16 :, :] = jnp.zeros((padded.shape[0] - CELLS - 16, LANES), F32)
    for m in range(CHILD):
        families[:, m * DOF : (m + 1) * DOF] = padded[pl.ds(head + m, FAMILIES, stride=CHILD), :][:, :DOF]
    f_hi, f_lo = split(families[:, : CHILD * DOF])
    r_hi = recon_hi[0 : CHILD * DOF, :]
    rebuilt[:, : CHILD * DOF] = dot_nt(f_hi, r_hi) + dot_nt(f_lo, r_hi) + dot_nt(f_hi, recon_lo[0 : CHILD * DOF, :])
    lane = lax.broadcasted_iota(I32, (FAMILIES, LANES), 1)
    for m in range(CHILD):
        part = rebuilt[:, m * DOF : m * DOF + LANES]
        padded[pl.ds(m, FAMILIES, stride=CHILD), :] = jnp.where(lane < DOF, part, 0.0)

    def cut(i, carry):
        at = pl.multiple_of(i * 8, 8)
        w_t[pl.ds(at, 8), :] = jnp.where(row + at < live, padded[pl.ds(at + 8 - head, 8), :], 0.0)
        return carry

    lax.fori_loop(0, CELLS // 8, cut, 0, unroll=8)


def kernel(counts, send, primal_in, dual_in, load_in, size_in, send_in, cell_in, other_in, dir_in, hanging_in,
           stiffness_in, recon_in, traction_in, trace_in,
           indicator, facts,
           primal, dual, load, cell_size, send_v, face_cell, face_other, face_dir, hanging, stiffness, recon, traction,
           trace, p_t, d_t, w_t, first, last, before, after, after2, p_out, p_in, w_out, w_in, padded, families, rebuilt,
           operator, table, side_a, side_b0, side_b1, recon_hi, recon_lo, index_a, index_b, smem_a, smem_b, term, partial, returned, part, parts,
           in_sem, index_sem, edge_send, edge_recv, p_send, p_recv, w_send, w_recv, b_send, b_recv, r_send, r_recv):
    me = lax.axis_index("dom")
    staged = [(dual_in, dual), (primal_in, primal), (recon_in, recon.at[pl.ds(0, CHILD * DOF), :]), (traction_in, traction), (trace_in, trace),
              (load_in, load), (size_in, cell_size), (stiffness_in, stiffness), (cell_in, face_cell),
              (other_in, face_other), (dir_in, face_dir), (hanging_in, hanging), (send_in, send_v)]
    loads = {}
    for i, (source, to) in enumerate(staged):
        loads[i] = pltpu.make_async_copy(source, to, in_sem.at[i])
        loads[i].start()

    barrier = pltpu.get_barrier_semaphore()
    partners = [behind(me, shift) for shift in SHIFTS]
    for stride, size in STAGES:
        partners += [in_stage(me, stride, size, step) for step in range(1, size)]
    for partner in partners:
        pl.semaphore_signal(barrier, inc=1, device_id=(partner,), device_id_type=MESH)

    start, live = counts_of(counts, me)
    head = lax.rem(CHILD - lax.rem(start, CHILD), CHILD)

    def remote(source, to, send_sem, recv_sem, target):
        return pltpu.make_async_remote_copy(src_ref=source, dst_ref=to, send_sem=send_sem, recv_sem=recv_sem,
                                            device_id=(target,), device_id_type=MESH)

    def list_copy(source, to, send_sem, recv_sem, k):
        return remote(source.at[k], to.at[k], send_sem.at[k], recv_sem.at[k], behind(me, shift_of(k)))

    loads[0].wait()

    def transpose_dual(step, carry):
        to_cell_major(d_t, dual, step)
        return carry

    lax.fori_loop(0, 8, transpose_dual, 0)
    first[...] = d_t[0:8, :]
    last[...] = d_t[pl.ds(jnp.maximum(live, 8) - 8, 8), :]
    pl.semaphore_wait(barrier, len(partners))
    edges = [remote(last, before, edge_send.at[0], edge_recv.at[0], behind(me, 1)),
             remote(first, after, edge_send.at[1], edge_recv.at[1], behind(me, -1))]
    for copy in edges:
        copy.start()

    def transpose_primal(step, carry):
        to_cell_major(p_t, primal, step)
        return carry

    loads[1].wait()
    lax.fori_loop(0, 8, transpose_primal, 0)

    def send_primal(step, carry):
        k = lax.rem(step + FIRST_LIST, NEIGH)
        gather_list(p_out, p_t, send, k)
        rows = pl.ds(pl.multiple_of(step * 96, 96), 96)
        recon_hi[rows, :], recon_lo[rows, :] = split(recon[rows, :])
        list_copy(p_out, p_in, p_send, p_recv, k).start()
        return carry

    loads[2].wait()
    lax.fori_loop(0, NEIGH, send_primal, 0)
    for copy in edges:
        copy.wait()
    rebuild(head, live, d_t, before, after, recon_hi, recon_lo, w_t, padded, families, rebuilt, after2)

    for i in range(3, len(staged)):
        loads[i].wait()
    fill_operator(operator, traction, trace)
    pair = (face_dir[...] // 2) * SLOTS
    index_a[...] = pair + face_cell[...]
    index_b[...] = pair + face_other[...]
    copy_a = pltpu.make_async_copy(index_a, smem_a, index_sem.at[0])
    copy_b = pltpu.make_async_copy(index_b, smem_b, index_sem.at[1])
    copy_a.start()
    copy_b.start()
    def send_weight(step, carry):
        k = lax.rem(step + FIRST_LIST, NEIGH)
        at = pl.multiple_of(step * 256, 256)
        gather_list(w_out, w_t, send, k)
        fill_table(table, at, p_t.at[pl.ds(at, 256), :], w_t.at[pl.ds(at, 256), :], operator)
        cell_terms(term, primal, load, w_t, cell_size, stiffness, step)
        list_copy(w_out, w_in, w_send, w_recv, k).start()
        return carry

    lax.fori_loop(0, NEIGH, send_weight, 0)
    copy_a.wait()
    copy_b.wait()

    def take_ghosts(step, carry):
        k = lax.rem(step + FIRST_LIST, NEIGH)
        list_copy(p_out, p_in, p_send, p_recv, k).wait()
        list_copy(w_out, w_in, w_send, w_recv, k).wait()
        row = step * 6
        gather_rows(side_a, row * LANES, table, lambda i: smem_a[row + i // LANES, i % LANES], 256)
        fill_table(table, CELLS + k * GHOST, p_in.at[k], w_in.at[k], operator)

        def rest(r, carry):
            gather_rows(side_a, r * LANES, table, lambda i: smem_a[r, i], LANES)
            return carry

        lax.fori_loop(row + 2, row + 6, rest, 0)
        return carry

    lax.fori_loop(0, NEIGH, take_ghosts, 0)

    lane = lax.broadcasted_iota(I32, (8, 2 * LANES), 1) % LANES
    sub = lax.broadcasted_iota(I32, (8, 2 * LANES), 0)
    pick = jnp.where(lane // 32 == sub, 1.0, 0.0).astype(BF16)
    upper = lax.broadcasted_iota(I32, (CHUNK, LANES), 1) % 64 >= 32

    def gather_b(to, c):
        gather_rows(to, 0, table, lambda i: smem_b[c * SPLIT + i // LANES, i % LANES], CHUNK)

    def raw_sums(side_b, c):
        a = side_a[pl.ds(pl.multiple_of(c * CHUNK, CHUNK), CHUNK), :]
        b = pltpu.roll(side_b[...], 64, 1)
        jump = pltpu.roll(a + b, 32, 1)
        hi, lo = split(jnp.where(upper, jump * a, pltpu.roll(jump * b, 96, 1)))
        return dot_nt(pick, jnp.concatenate([hi, lo], 1))

    def add_sums(raw, c, carry):
        sum_a, sum_b = carry
        face = c * CHUNK + lax.broadcasted_iota(I32, (1, CHUNK), 1)
        area = jnp.where(face < 3 * live, 0.5 * (1.0 - 0.75 * lanes_of(hanging, c).astype(F32)), 0.0)
        is_even = lanes_of(face_dir, c) % 2 == 0
        term_a = area * jnp.where(is_even, raw[1:2], raw[3:4])
        term_b = area * jnp.where(is_even, raw[0:1], raw[2:3])
        sum_a += scatter(lanes_of(face_cell, c), term_a, CELLS // LANES)
        sum_b += scatter(lanes_of(face_other, c), term_b, SLOTS // LANES)
        return sum_a, sum_b

    def body(i, carry):
        raw_before, sums = carry
        gather_b(side_b1, 2 * i + 1)
        raw = raw_sums(side_b0, 2 * i)
        sums = add_sums(raw_before, jnp.maximum(2 * i - 1, 0), sums)
        gather_b(side_b0, jnp.minimum(2 * i + 2, CHUNKS - 1))
        raw_after = raw_sums(side_b1, 2 * i + 1)
        sums = add_sums(raw, 2 * i, sums)
        return raw_after, sums

    gather_b(side_b0, 0)
    zero = (jnp.zeros((CELLS // LANES, LANES), F32), jnp.zeros((SLOTS // LANES, LANES), F32))
    raw, sums = lax.fori_loop(0, CHUNKS // 2, body, (jnp.zeros((8, CHUNK), F32), zero))
    sum_a, sum_b = add_sums(raw, CHUNKS - 1, sums)
    backs = []
    for k in range(NEIGH):
        at = CELLS // LANES + 2 * k
        partial[k, 0:2, :] = sum_b[at : at + 2]
        backs.append(remote(partial.at[k], returned.at[k], b_send.at[k], b_recv.at[k], behind(me, -SHIFTS[k])))
        backs[-1].start()
    for copy in backs:
        copy.wait()
    index = jnp.concatenate([send_v[k : k + 1, :] for k in range(NEIGH)], 1)
    value = jnp.concatenate([returned[k, r : r + 1, :] for k in range(NEIGH) for r in range(2)], 1)
    out = term[...] + sum_a + sum_b[: CELLS // LANES] + scatter(index, value, CELLS // LANES)
    slot = lax.broadcasted_iota(I32, out.shape, 0) * LANES + lax.broadcasted_iota(I32, out.shape, 1)
    indicator[...] = out

    size = jnp.where(slot < live, jnp.abs(out), 0.0)
    total = size[0:8] + size[8:16]
    place = 0
    for stage, (stride, count) in enumerate(STAGES):
        part[stage] = total
        copies = []
        for step in range(1, count):
            copies.append(remote(part.at[stage], parts.at[place + step - 1], r_send.at[place + step - 1],
                                 r_recv.at[place + step - 1], in_stage(me, stride, count, step)))
            copies[-1].start()
        for step in range(1, count):
            copies[step - 1].wait()
            total += parts[place + step - 1]
        place += count - 1

    def all_cells(i, carry):
        return carry + counts[i]

    cells = lax.fori_loop(0, RANKS, all_cells, jnp.int32(0), unroll=8)
    mean = jnp.sum(total) / cells.astype(F32)
    facts[...] = jnp.where(slot < live, mean, -1.0)


SMEM = pl.BlockSpec(memory_space=pltpu.SMEM)
VMEM = pl.BlockSpec(memory_space=pltpu.VMEM)
ANY = pl.BlockSpec(memory_space=pl.ANY)


def per_device(primal, dual, load, cell_size, cell_count, ghost_send, face_cell, face_other, face_dir, hanging,
               stiffness, recon, traction, trace):
    send = ghost_send[0]
    as_rows = lambda x: x.reshape(-1, LANES)
    f32 = lambda *shape: pltpu.VMEM(shape, F32)
    i32 = lambda *shape: pltpu.VMEM(shape, I32)
    dma = lambda n: pltpu.SemaphoreType.DMA((n,))
    rows = FACES // LANES
    cells = CELLS // LANES
    steps = sum(size - 1 for _, size in STAGES)
    scratch = [
        f32(DOF, CELLS), f32(DOF, CELLS), f32(DOF, CELLS), f32(cells, LANES), i32(NEIGH, GHOST),
        i32(rows, LANES), i32(rows, LANES), i32(rows, LANES), i32(rows, LANES),
        f32(DOF, DOF), f32(768, CHILD * DOF), f32(6 * FACE_DOF, DOF), f32(6 * FACE_DOF, DOF),
        f32(CELLS, LANES), f32(CELLS, LANES), f32(CELLS, LANES),
        f32(8, LANES), f32(8, LANES), f32(8, LANES), f32(8, LANES), f32(16, LANES),
        f32(NEIGH, GHOST, LANES), f32(NEIGH, GHOST, LANES), f32(NEIGH, GHOST, LANES), f32(NEIGH, GHOST, LANES),
        f32(FAMILIES * CHILD + 8, LANES), f32(FAMILIES, 768), f32(FAMILIES, 768),
        f32(384, 256), f32(3 * SLOTS, LANES), f32(FACES, LANES), f32(CHUNK, LANES), f32(CHUNK, LANES),
        pltpu.VMEM((768, CHILD * DOF), BF16), pltpu.VMEM((768, CHILD * DOF), BF16),
        i32(rows, LANES), i32(rows, LANES), pltpu.SMEM((rows, LANES), I32), pltpu.SMEM((rows, LANES), I32),
        f32(cells, LANES), f32(NEIGH, 8, LANES), f32(NEIGH, 8, LANES), f32(len(STAGES), 8, LANES), f32(steps, 8, LANES),
        dma(13), dma(2), dma(2), dma(2), dma(NEIGH), dma(NEIGH), dma(NEIGH), dma(NEIGH), dma(NEIGH), dma(NEIGH),
        dma(steps), dma(steps),
    ]
    indicator, facts = pl.pallas_call(
        kernel,
        out_shape=[jax.ShapeDtypeStruct((cells, LANES), F32)] * 2,
        in_specs=[SMEM] * 2 + [ANY] * 13, out_specs=[VMEM] * 2, scratch_shapes=scratch,
        compiler_params=pltpu.CompilerParams(collective_id=0, has_side_effects=True,
                                             vmem_limit_bytes=56 * 1024 * 1024),
        name="indicators",
    )(cell_count, send, primal, dual, load, as_rows(cell_size), send, as_rows(face_cell), as_rows(face_other),
      as_rows(face_dir), as_rows(hanging), stiffness, recon, traction, trace)
    facts = facts.reshape(-1)
    indicator = jnp.where(facts < 0.0, 0.0, indicator.reshape(-1))
    return indicator, jnp.abs(indicator) / (jnp.abs(facts) + 1e-06)

def solution(mesh):
    in_specs = (P(None, "dom"), P(None, "dom"), P(None, "dom"), P("dom"), P(), P("dom", None, None), P("dom"), P("dom"),
                P("dom"), P("dom"), P(), P(), P(), P())
    return jax.shard_map(per_device, mesh=mesh, in_specs=in_specs, out_specs=(P("dom"), P("dom")), check_vma=False)
```

time: 412 us -> 63.3 us (0.15)
  local copies, waits for them, and re-layouts: 110 us -> 0 us
  other arithmetic: 111 us -> 1.32 us
  blocking collectives: 94.5 us -> 0 us
  Pallas kernels: 0 us -> 60.9 us
  starting transfers between devices: 52.8 us -> 0 us
  matrix products: 28.2 us -> 0 us
  waiting for transfers between devices: 7.96 us -> 0 us
  between operations: 5.95 us -> 0.64 us
    psum x1 -> x0, blocking collectives: 94.5 us -> none  [per_device(): abs_sum = lax.psum(jnp.sum(jnp.abs(indicator)), 'dom')]
    scatter-add x3 -> x0, other arithmetic: 92.6 us -> none  [the longest x2 77.9 us: per_device(): face_sums = jnp.zeros((extended.shape[1],), jnp.float32).at[face_cell].ad...]
    gather x3 -> x0, local copies, waits for them, and re-layouts: 62 us -> none  [the longest x1 25.9 us: per_device(): side_a = extended[:, face_cell]]
    pallas_call x0 -> x1, Pallas kernels: none -> 60.9 us  [per_device(): pl.pallas_call(kernel, out_shape=[jax.ShapeDtypeStruct((cells, LANES), F3...]
    ppermute x18 -> x0, starting transfers between devices: 52.8 us -> none  [from_behind(): return lax.ppermute(shard, axis, pairs)]
    dot_general x6 -> x0, matrix products: 28.2 us -> none  [the longest x1 7.68 us: per_device(): jnp.dot(traction, side_a[:node_rows], precision=precise, preferred_elemen...]
    reshape x8 -> x0, local copies, waits for them, and re-layouts: 24.4 us -> none  [the longest x4 19.4 us: pick_direction(): dir_table = all_rows.reshape(DIRS, FACE_DOF, width_cols)]
    reduce_sum x4 -> x0, other arithmetic: 10.9 us -> none  [the longest x1 7.9 us: pick_direction(): return jnp.sum(dir_table * onehot[:, None, :], axis=0)]
  transfers between devices with their start and end apart: 18 -> 0, of which waited for: 3 -> 0; matrix products, arithmetic and copies ran while one was open for 2% -> 0% of each run, Pallas kernels for 0% -> 0%
where the time goes in v1:
time: 63.3 us; the launch traced here: 62.9 us
  Pallas kernels  60.9 us (96%)
  other arithmetic  1.32 us (2%)
  between operations  0.64 us (1%)
    pallas_call x1, Pallas kernels, per_device(): pl.pallas_call(kernel, out_shape=[jax.ShapeDtypeStruct((cells, LANES), F3...  60.9 us
    div x1, other arithmetic, per_device(): return (indicator, jnp.abs(indicator) / (jnp.abs(facts) + 1e-06))  1.32 us

profile of v1, /device:TPU:0, one launch (start us, length us, event | category | flops | bytes accessed | tf_op | source)
XLA Modules:
  0.0 62.9 jit_solution(6382724193037049134)
XLA Ops:
  0.6 60.9 %indicators.1 = (f32[16,128]{1,0:T(8,128)}, f32[16,128]{1,0:T(8,128)}) custom-call(s32[128]{0:T(128)} %counts.1, s32[8,256]{1,0:T(8,128)} %bitcast.11, f32[81,2048]{1,0:T(8,128)} %primal_in.1, f32[81,2048]{1,0:T(8,128)} %dual_in.1, f32[81,2048]{1,0:T(8,128)} %load_in.1, f32[16,128]{1,0:T(8,128)} %bitcast.17, s32[8,256]{1,0:T(8,128)} %bitcast.12, ...), custom_call_target="tpu_custom_call" | custom-call | tf_op jit(solution)/shard_map/indicators/pallas_call | solution.py:388
  61.6 1.3 %bitcast_divide_fusion = (f32[2048]{0:T(1024)}, f32[2048]{0:T(1024)}) fusion(f32[16,128]{1,0:T(8,128)} %get-tuple-element.4, f32[16,128]{1,0:T(8,128)} %get-tuple-element.5), kind=kLoop, calls=%fused_computation | loop fusion | flops 12288 | bytes 32768 | tf_op jit(solution)/shard_map/div | solution.py:399

commit v2 on v1

--- a/solution.py
+++ b/solution.py
@@ -42,8 +42,9 @@
 
 
 def gather_rows(dst, dst_at, src, index_of, count):
+    src = src.reshape(src.shape[0], 1, LANES)
     for base in range(0, count, BATCH):
-        rows = [src[pl.ds(index_of(base + u), 1), :] for u in range(BATCH)]
+        rows = [src[index_of(base + u)] for u in range(BATCH)]
         for u in range(BATCH):
             dst[pl.ds(dst_at + (base + u), 1), :] = rows[u]
 
@@ -248,6 +249,7 @@
     copy_b = pltpu.make_async_copy(index_b, smem_b, index_sem.at[1])
     copy_a.start()
     copy_b.start()
+
     def send_weight(step, carry):
         k = lax.rem(step + FIRST_LIST, NEIGH)
         at = pl.multiple_of(step * 256, 256)

time: 63.3 us -> 63.3 us (level)
  no operation moved by 1% of the time
where the time goes in v2:
time: 63.3 us; the launch traced here: 62.9 us
  Pallas kernels  60.9 us (96%)
  other arithmetic  1.32 us (2%)
  between operations  0.64 us (1%)
    pallas_call x1, Pallas kernels, per_device(): pl.pallas_call(kernel, out_shape=[jax.ShapeDtypeStruct((cells, LANES), F3...  60.9 us
    div x1, other arithmetic, per_device(): return (indicator, jnp.abs(indicator) / (jnp.abs(facts) + 1e-06))  1.32 us

profile of v2, /device:TPU:0, one launch (start us, length us, event | category | flops | bytes accessed | tf_op | source)
XLA Modules:
  0.0 62.9 jit_solution(6382724193037049134)
XLA Ops:
  0.6 60.9 %indicators.1 = (f32[16,128]{1,0:T(8,128)}, f32[16,128]{1,0:T(8,128)}) custom-call(s32[128]{0:T(128)} %counts.1, s32[8,256]{1,0:T(8,128)} %bitcast.11, f32[81,2048]{1,0:T(8,128)} %primal_in.1, f32[81,2048]{1,0:T(8,128)} %dual_in.1, f32[81,2048]{1,0:T(8,128)} %load_in.1, f32[16,128]{1,0:T(8,128)} %bitcast.17, s32[8,256]{1,0:T(8,128)} %bitcast.12, ...), custom_call_target="tpu_custom_call" | custom-call | tf_op jit(solution)/shard_map/indicators/pallas_call | solution.py:390
  61.6 1.3 %bitcast_divide_fusion = (f32[2048]{0:T(1024)}, f32[2048]{0:T(1024)}) fusion(f32[16,128]{1,0:T(8,128)} %get-tuple-element.4, f32[16,128]{1,0:T(8,128)} %get-tuple-element.5), kind=kLoop, calls=%fused_computation | loop fusion | flops 12288 | bytes 32768 | tf_op jit(solution)/shard_map/div | solution.py:401

commit v3 on v1

--- a/solution.py
+++ b/solution.py
@@ -22,7 +22,9 @@
 FACES = 6144
 LANES = 128
 BATCH = 16
-FAMILIES = 264
+FAMILIES = 272
+THIRD = 88
+PACKED = 2 * THIRD
 CHUNK = 256
 CHUNKS = FACES // CHUNK
 SPLIT = CHUNK // LANES
@@ -55,6 +57,22 @@
 def to_cell_major(dst, src, step):
     at = pl.multiple_of(step * 256, 256)
     dst[pl.ds(at, 256), :] = turned_block(src, at)
+
+
+def pack(to, rows):
+    lane = lax.broadcasted_iota(I32, (THIRD, LANES), 1)
+    second = pltpu.roll(rows[THIRD : 2 * THIRD, :], DOF, 1)
+    third = pltpu.roll(rows[2 * THIRD :, :], 2 * DOF - LANES, 1)
+    upper = jnp.where(lane < DOF, rows[0:THIRD, :], second)
+    to[...] = jnp.concatenate([upper, jnp.where(lane < 2 * DOF - LANES, second, third)], 0)
+
+
+def unpack(rows):
+    lane = lax.broadcasted_iota(I32, (THIRD, LANES), 1)
+    upper, lower = rows[:THIRD], rows[THIRD:]
+    second = pltpu.roll(jnp.where(lane < 2 * DOF - LANES, lower, upper), LANES - DOF, 1)
+    third = pltpu.roll(lower, 2 * LANES - 2 * DOF, 1)
+    return jnp.concatenate([upper, second, third[: GHOST - PACKED]], 0)
 
 
 def fill_operator(operator, traction, trace):
@@ -67,19 +85,22 @@
 
 def fill_table(table, slot, p_rows, w_rows, operator):
     o_hi, o_lo = split(operator[...])
-    x_hi, x_lo = split(jnp.concatenate([p_rows[...], w_rows[...]], 1))
+    x_hi, x_lo = split(jnp.concatenate([p_rows, w_rows], 1))
     out = dot_nt(x_hi, o_hi) + dot_nt(x_lo, o_hi) + dot_nt(x_hi, o_lo)
     for pair in range(3):
         table[pl.ds(pl.multiple_of(pair * SLOTS + slot, 256), 256), :] = out[:, pair * LANES : (pair + 1) * LANES]
 
 
-def cell_terms(out, primal, load, w_t, cell_size, stiffness, step):
-    at = pl.multiple_of(step * 256, 256)
+def take_residual(load, primal, stiffness, step):
+    cells = pl.ds(pl.multiple_of(step * 256, 256), 256)
     s_hi, s_lo = split(stiffness[...])
-    p_hi, p_lo = split(primal[:, pl.ds(at, 256)])
-    residual = load[:, pl.ds(at, 256)] - (dot_nn(s_hi, p_hi) + dot_nn(s_lo, p_hi) + dot_nn(s_hi, p_lo))
-    weight = w_t[pl.ds(at, 256), :].T[:DOF, :]
-    total = jnp.sum(residual * weight, axis=0, keepdims=True)
+    p_hi, p_lo = split(primal[:, cells])
+    load[:, cells] = load[:, cells] - (dot_nn(s_hi, p_hi) + dot_nn(s_lo, p_hi) + dot_nn(s_hi, p_lo))
+
+
+def cell_terms(out, residual, w_t, cell_size, step):
+    cells = pl.ds(pl.multiple_of(step * 256, 256), 256)
+    total = jnp.sum(residual[:, cells] * w_t[cells, :].T[:DOF, :], axis=0, keepdims=True)
     for r in range(2):
         i = step * 2 + r
         out[pl.ds(i, 1), :] = cell_size[pl.ds(i, 1), :] * total[:, r * LANES : (r + 1) * LANES]
@@ -131,8 +152,8 @@
     return me + (lax.rem(place + step, size) - place) * stride
 
 
-def gather_list(ghosts, source, send, k):
-    gather_rows(ghosts.at[k], 0, source, lambda i: send[k, i], GHOST)
+def gather_list(picked, source, send, k):
+    gather_rows(picked, 0, source, lambda i: send[k, i], GHOST)
 
 
 def rebuild(head, live, d_t, before, after, recon_hi, recon_lo, w_t, padded, families, rebuilt, after2):
@@ -155,7 +176,8 @@
         families[:, m * DOF : (m + 1) * DOF] = padded[pl.ds(head + m, FAMILIES, stride=CHILD), :][:, :DOF]
     f_hi, f_lo = split(families[:, : CHILD * DOF])
     r_hi = recon_hi[0 : CHILD * DOF, :]
-    rebuilt[:, : CHILD * DOF] = dot_nt(f_hi, r_hi) + dot_nt(f_lo, r_hi) + dot_nt(f_hi, recon_lo[0 : CHILD * DOF, :])
+    both = dot_nt(jnp.concatenate([f_hi, f_lo], 0), r_hi)
+    rebuilt[:, : CHILD * DOF] = both[:FAMILIES] + both[FAMILIES:] + dot_nt(f_hi, recon_lo[0 : CHILD * DOF, :])
     lane = lax.broadcasted_iota(I32, (FAMILIES, LANES), 1)
     for m in range(CHILD):
         part = rebuilt[:, m * DOF : m * DOF + LANES]
@@ -173,11 +195,11 @@
            stiffness_in, recon_in, traction_in, trace_in,
            indicator, facts,
            primal, dual, load, cell_size, send_v, face_cell, face_other, face_dir, hanging, stiffness, recon, traction,
-           trace, p_t, d_t, w_t, first, last, before, after, after2, p_out, p_in, w_out, w_in, padded, families, rebuilt,
+           trace, p_t, d_t, w_t, first, last, before, after, after2, p_out, p_in, w_out, w_in, picked, padded, families, rebuilt,
            operator, table, side_a, side_b0, side_b1, recon_hi, recon_lo, index_a, index_b, smem_a, smem_b, term, partial, returned, part, parts,
            in_sem, index_sem, edge_send, edge_recv, p_send, p_recv, w_send, w_recv, b_send, b_recv, r_send, r_recv):
     me = lax.axis_index("dom")
-    staged = [(dual_in, dual), (primal_in, primal), (recon_in, recon.at[pl.ds(0, CHILD * DOF), :]), (traction_in, traction), (trace_in, trace),
+    staged = [(primal_in, primal), (recon_in, recon.at[pl.ds(0, CHILD * DOF), :]), (dual_in, dual), (traction_in, traction), (trace_in, trace),
               (load_in, load), (size_in, cell_size), (stiffness_in, stiffness), (cell_in, face_cell),
               (other_in, face_other), (dir_in, face_dir), (hanging_in, hanging), (send_in, send_v)]
     loads = {}
@@ -204,39 +226,32 @@
 
     loads[0].wait()
 
-    def transpose_dual(step, carry):
+    def transpose_primal(step, carry):
+        to_cell_major(p_t, primal, step)
+        rows = pl.ds(pl.multiple_of(step * 96, 96), 96)
+        recon_hi[rows, :], recon_lo[rows, :] = split(recon[rows, :])
+        return carry
+
+    loads[1].wait()
+    lax.fori_loop(0, 8, transpose_primal, 0)
+    loads[2].wait()
+    pl.semaphore_wait(barrier, len(partners))
+
+    def send_primal(step, carry):
+        k = lax.rem(step + FIRST_LIST, NEIGH)
+        gather_list(picked, p_t, send, k)
         to_cell_major(d_t, dual, step)
-        return carry
-
-    lax.fori_loop(0, 8, transpose_dual, 0)
+        pack(p_out.at[k], picked)
+        list_copy(p_out, p_in, p_send, p_recv, k).start()
+        return carry
+
+    lax.fori_loop(0, NEIGH, send_primal, 0)
     first[...] = d_t[0:8, :]
     last[...] = d_t[pl.ds(jnp.maximum(live, 8) - 8, 8), :]
-    pl.semaphore_wait(barrier, len(partners))
     edges = [remote(last, before, edge_send.at[0], edge_recv.at[0], behind(me, 1)),
              remote(first, after, edge_send.at[1], edge_recv.at[1], behind(me, -1))]
     for copy in edges:
         copy.start()
-
-    def transpose_primal(step, carry):
-        to_cell_major(p_t, primal, step)
-        return carry
-
-    loads[1].wait()
-    lax.fori_loop(0, 8, transpose_primal, 0)
-
-    def send_primal(step, carry):
-        k = lax.rem(step + FIRST_LIST, NEIGH)
-        gather_list(p_out, p_t, send, k)
-        rows = pl.ds(pl.multiple_of(step * 96, 96), 96)
-        recon_hi[rows, :], recon_lo[rows, :] = split(recon[rows, :])
-        list_copy(p_out, p_in, p_send, p_recv, k).start()
-        return carry
-
-    loads[2].wait()
-    lax.fori_loop(0, NEIGH, send_primal, 0)
-    for copy in edges:
-        copy.wait()
-    rebuild(head, live, d_t, before, after, recon_hi, recon_lo, w_t, padded, families, rebuilt, after2)
 
     for i in range(3, len(staged)):
         loads[i].wait()
@@ -248,12 +263,23 @@
     copy_b = pltpu.make_async_copy(index_b, smem_b, index_sem.at[1])
     copy_a.start()
     copy_b.start()
+
+    def residuals(step, carry):
+        take_residual(load, primal, stiffness, step)
+        return carry
+
+    lax.fori_loop(0, 8, residuals, 0)
+    for copy in edges:
+        copy.wait()
+    rebuild(head, live, d_t, before, after, recon_hi, recon_lo, w_t, padded, families, rebuilt, after2)
+
     def send_weight(step, carry):
         k = lax.rem(step + FIRST_LIST, NEIGH)
         at = pl.multiple_of(step * 256, 256)
-        gather_list(w_out, w_t, send, k)
-        fill_table(table, at, p_t.at[pl.ds(at, 256), :], w_t.at[pl.ds(at, 256), :], operator)
-        cell_terms(term, primal, load, w_t, cell_size, stiffness, step)
+        gather_list(picked, w_t, send, k)
+        fill_table(table, at, p_t[pl.ds(at, 256), :], w_t[pl.ds(at, 256), :], operator)
+        cell_terms(term, load, w_t, cell_size, step)
+        pack(w_out.at[k], picked)
         list_copy(w_out, w_in, w_send, w_recv, k).start()
         return carry
 
@@ -267,7 +293,7 @@
         list_copy(w_out, w_in, w_send, w_recv, k).wait()
         row = step * 6
         gather_rows(side_a, row * LANES, table, lambda i: smem_a[row + i // LANES, i % LANES], 256)
-        fill_table(table, CELLS + k * GHOST, p_in.at[k], w_in.at[k], operator)
+        fill_table(table, CELLS + k * GHOST, unpack(p_in[k]), unpack(w_in[k]), operator)
 
         def rest(r, carry):
             gather_rows(side_a, r * LANES, table, lambda i: smem_a[r, i], LANES)
@@ -376,7 +402,8 @@
         f32(DOF, DOF), f32(768, CHILD * DOF), f32(6 * FACE_DOF, DOF), f32(6 * FACE_DOF, DOF),
         f32(CELLS, LANES), f32(CELLS, LANES), f32(CELLS, LANES),
         f32(8, LANES), f32(8, LANES), f32(8, LANES), f32(8, LANES), f32(16, LANES),
-        f32(NEIGH, GHOST, LANES), f32(NEIGH, GHOST, LANES), f32(NEIGH, GHOST, LANES), f32(NEIGH, GHOST, LANES),
+        f32(NEIGH, PACKED, LANES), f32(NEIGH, PACKED, LANES), f32(NEIGH, PACKED, LANES), f32(NEIGH, PACKED, LANES),
+        f32(3 * THIRD, LANES),
         f32(FAMILIES * CHILD + 8, LANES), f32(FAMILIES, 768), f32(FAMILIES, 768),
         f32(384, 256), f32(3 * SLOTS, LANES), f32(FACES, LANES), f32(CHUNK, LANES), f32(CHUNK, LANES),
         pltpu.VMEM((768, CHILD * DOF), BF16), pltpu.VMEM((768, CHILD * DOF), BF16),

time: 63.3 us -> 63.9 us (level)
  no operation moved by 1% of the time
where the time goes in v3:
time: 63.9 us; the launch traced here: 63.2 us
  Pallas kernels  61.2 us (96%)
  other arithmetic  1.32 us (2%)
  between operations  0.64 us (1%)
    pallas_call x1, Pallas kernels, per_device(): pl.pallas_call(kernel, out_shape=[jax.ShapeDtypeStruct((cells, LANES), F3...  61.2 us
    div x1, other arithmetic, per_device(): return (indicator, jnp.abs(indicator) / (jnp.abs(facts) + 1e-06))  1.32 us

profile of v3, /device:TPU:0, one launch (start us, length us, event | category | flops | bytes accessed | tf_op | source)
XLA Modules:
  0.0 63.2 jit_solution(6196582930195666607)
XLA Ops:
  0.6 61.2 %indicators.1 = (f32[16,128]{1,0:T(8,128)}, f32[16,128]{1,0:T(8,128)}) custom-call(s32[128]{0:T(128)} %counts.1, s32[8,256]{1,0:T(8,128)} %bitcast.11, f32[81,2048]{1,0:T(8,128)} %primal_in.1, f32[81,2048]{1,0:T(8,128)} %dual_in.1, f32[81,2048]{1,0:T(8,128)} %load_in.1, f32[16,128]{1,0:T(8,128)} %bitcast.17, s32[8,256]{1,0:T(8,128)} %bitcast.12, ...), custom_call_target="tpu_custom_call" | custom-call | tf_op jit(solution)/shard_map/indicators/pallas_call | solution.py:415
  61.8 1.3 %bitcast_divide_fusion = (f32[2048]{0:T(1024)}, f32[2048]{0:T(1024)}) fusion(f32[16,128]{1,0:T(8,128)} %get-tuple-element.4, f32[16,128]{1,0:T(8,128)} %get-tuple-element.5), kind=kLoop, calls=%fused_computation | loop fusion | flops 12288 | bytes 32768 | tf_op jit(solution)/shard_map/div | solution.py:426

commit v4 on v3

--- a/solution.py
+++ b/solution.py
@@ -21,7 +21,7 @@
 SLOTS = CELLS + GHOSTS
 FACES = 6144
 LANES = 128
-BATCH = 16
+LAG = 16
 FAMILIES = 272
 THIRD = 88
 PACKED = 2 * THIRD
@@ -44,19 +44,21 @@
 
 
 def gather_rows(dst, dst_at, src, index_of, count):
-    for base in range(0, count, BATCH):
-        rows = [src[pl.ds(index_of(base + u), 1), :] for u in range(BATCH)]
-        for u in range(BATCH):
-            dst[pl.ds(dst_at + (base + u), 1), :] = rows[u]
+    held = []
+    for i in range(count + LAG):
+        if i < count:
+            held.append(src[pl.ds(index_of(i), 1), :])
+        if i >= LAG:
+            dst[pl.ds(dst_at + (i - LAG), 1), :] = held[i - LAG]
 
 
 def turned_block(src, at):
     return jnp.concatenate([src[:, pl.ds(at, 256)], jnp.zeros((LANES - DOF, 256), F32)], 0).T
 
 
-def to_cell_major(dst, src, step):
+def to_cell_major(dst, row, src, step):
     at = pl.multiple_of(step * 256, 256)
-    dst[pl.ds(at, 256), :] = turned_block(src, at)
+    dst[pl.ds(pl.multiple_of(row + at, CHILD), 256), :] = turned_block(src, at)
 
 
 def pack(to, rows):
@@ -84,9 +86,8 @@
 
 
 def fill_table(table, slot, p_rows, w_rows, operator):
-    o_hi, o_lo = split(operator[...])
-    x_hi, x_lo = split(jnp.concatenate([p_rows, w_rows], 1))
-    out = dot_nt(x_hi, o_hi) + dot_nt(x_lo, o_hi) + dot_nt(x_hi, o_lo)
+    hi, lo = split(jnp.concatenate([p_rows, w_rows], 1))
+    out = dot_nn(jnp.concatenate([hi, lo, hi], 1), operator[...])
     for pair in range(3):
         table[pl.ds(pl.multiple_of(pair * SLOTS + slot, 256), 256), :] = out[:, pair * LANES : (pair + 1) * LANES]
 
@@ -98,9 +99,9 @@
     load[:, cells] = load[:, cells] - (dot_nn(s_hi, p_hi) + dot_nn(s_lo, p_hi) + dot_nn(s_hi, p_lo))
 
 
-def cell_terms(out, residual, w_t, cell_size, step):
+def cell_terms(out, residual, woven, skip, cell_size, step):
     cells = pl.ds(pl.multiple_of(step * 256, 256), 256)
-    total = jnp.sum(residual[:, cells] * w_t[cells, :].T[:DOF, :], axis=0, keepdims=True)
+    total = jnp.sum(residual[:, cells] * woven[pl.ds(skip + step * 256, 256), :].T[:DOF, :], axis=0, keepdims=True)
     for r in range(2):
         i = step * 2 + r
         out[pl.ds(i, 1), :] = cell_size[pl.ds(i, 1), :] * total[:, r * LANES : (r + 1) * LANES]
@@ -110,14 +111,14 @@
     return jnp.concatenate([ref[pl.ds(chunk * SPLIT + i, 1), :] for i in range(SPLIT)], 1)
 
 
-def scatter(index, value, high_count):
-    width = index.shape[1]
-    high = index >> 7
-    low = index & 127
-    chosen = lax.broadcasted_iota(I32, (high_count, width), 0) == high
-    v_hi, v_lo = split(jnp.where(chosen, value, 0.0))
-    onehot = jnp.where(lax.broadcasted_iota(I32, (LANES, width), 0) == low, 1.0, 0.0).astype(BF16)
-    both = dot_nt(jnp.concatenate([v_hi, v_lo], 0), onehot)
+def low_onehot(index):
+    low = lax.broadcasted_iota(I32, (LANES, index.shape[1]), 0) == index % LANES
+    return jnp.where(low, 1.0, 0.0).astype(BF16)
+
+
+def scatter(index, value, high_count, onehot):
+    high = lax.broadcasted_iota(I32, (high_count, index.shape[1]), 0) == index // LANES
+    both = dot_nt(jnp.concatenate(split(jnp.where(high, value, 0.0)), 0), onehot)
     return both[:high_count] + both[high_count:]
 
 
@@ -130,11 +131,11 @@
 
 def counts_of(counts, me):
     def body(i, carry):
-        before, here = carry
+        before, here, cells = carry
         c = counts[i]
-        return before + jnp.where(i < me, c, 0), here + jnp.where(i == me, c, 0)
-
-    return lax.fori_loop(0, RANKS, body, (jnp.int32(0), jnp.int32(0)), unroll=8)
+        return before + jnp.where(i < me, c, 0), here + jnp.where(i == me, c, 0), cells + c
+
+    return lax.fori_loop(0, RANKS, body, (jnp.int32(0), jnp.int32(0), jnp.int32(0)), unroll=32)
 
 
 def behind(me, by):
@@ -156,47 +157,32 @@
     gather_rows(picked, 0, source, lambda i: send[k, i], GHOST)
 
 
-def rebuild(head, live, d_t, before, after, recon_hi, recon_lo, w_t, padded, families, rebuilt, after2):
-    after2[0:8, :] = after[...]
+def rebuild(head, live, padded, after, after2, recon3, families, rebuilt, woven):
+    after2[0:8, :] = jnp.zeros((8, LANES), F32)
     after2[8:16, :] = after[...]
-    turned = after2[pl.ds(8 - live % 8, 8), :]
-    row = lax.broadcasted_iota(I32, (8, LANES), 0)
-    padded[0:8, :] = before[...]
-
-    def fill(i, carry):
-        at = pl.multiple_of(i * 8, 8)
-        own = d_t[pl.ds(at, 8), :]
-        padded[pl.ds(at + 8, 8), :] = jnp.where(row + at < live, own, turned)
-        return carry
-
-    lax.fori_loop(0, CELLS // 8, fill, 0, unroll=8)
-    padded[CELLS + 8 : CELLS + 16, :] = turned
-    padded[CELLS + 16 :, :] = jnp.zeros((padded.shape[0] - CELLS - 16, LANES), F32)
+    own = lax.rem(live - head + CHILD, CHILD)
+    split_family = 1 + (live - head) // CHILD
+    row = lax.broadcasted_iota(I32, (FAMILIES, LANES), 0)
+    families[:, 640:768] = jnp.zeros((FAMILIES, LANES), F32)
     for m in range(CHILD):
-        families[:, m * DOF : (m + 1) * DOF] = padded[pl.ds(head + m, FAMILIES, stride=CHILD), :][:, :DOF]
-    f_hi, f_lo = split(families[:, : CHILD * DOF])
-    r_hi = recon_hi[0 : CHILD * DOF, :]
-    both = dot_nt(jnp.concatenate([f_hi, f_lo], 0), r_hi)
-    rebuilt[:, : CHILD * DOF] = both[:FAMILIES] + both[FAMILIES:] + dot_nt(f_hi, recon_lo[0 : CHILD * DOF, :])
+        cells = padded[pl.ds(head + m, FAMILIES, stride=CHILD), :]
+        late = after2[pl.ds(CHILD + m - own, 1), :]
+        cells = jnp.where((row == split_family) & (m >= own), late, cells)
+        families[:, m * DOF : (m + 1) * DOF] = cells[:, :DOF]
+    hi, lo = split(families[...])
+    rebuilt[:, : CHILD * DOF] = dot_nt(jnp.concatenate([hi, lo, hi], 1), recon3[0 : CHILD * DOF, :])
     lane = lax.broadcasted_iota(I32, (FAMILIES, LANES), 1)
     for m in range(CHILD):
         part = rebuilt[:, m * DOF : m * DOF + LANES]
-        padded[pl.ds(m, FAMILIES, stride=CHILD), :] = jnp.where(lane < DOF, part, 0.0)
-
-    def cut(i, carry):
-        at = pl.multiple_of(i * 8, 8)
-        w_t[pl.ds(at, 8), :] = jnp.where(row + at < live, padded[pl.ds(at + 8 - head, 8), :], 0.0)
-        return carry
-
-    lax.fori_loop(0, CELLS // 8, cut, 0, unroll=8)
+        woven[pl.ds(m, FAMILIES, stride=CHILD), :] = jnp.where(lane < DOF, part, 0.0)
 
 
 def kernel(counts, send, primal_in, dual_in, load_in, size_in, send_in, cell_in, other_in, dir_in, hanging_in,
            stiffness_in, recon_in, traction_in, trace_in,
            indicator, facts,
            primal, dual, load, cell_size, send_v, face_cell, face_other, face_dir, hanging, stiffness, recon, traction,
-           trace, p_t, d_t, w_t, first, last, before, after, after2, p_out, p_in, w_out, w_in, picked, padded, families, rebuilt,
-           operator, table, side_a, side_b0, side_b1, recon_hi, recon_lo, index_a, index_b, smem_a, smem_b, term, partial, returned, part, parts,
+           trace, p_t, first, last, before, after, after2, p_out, p_in, w_out, w_in, picked, padded, woven, families, rebuilt,
+           operator, operator3, table, side_a, side_b0, side_b1, recon3, onehot, index_a, index_b, smem_a, smem_b, term, partial, returned, part, parts,
            in_sem, index_sem, edge_send, edge_recv, p_send, p_recv, w_send, w_recv, b_send, b_recv, r_send, r_recv):
     me = lax.axis_index("dom")
     staged = [(primal_in, primal), (recon_in, recon.at[pl.ds(0, CHILD * DOF), :]), (dual_in, dual), (traction_in, traction), (trace_in, trace),
@@ -214,7 +200,7 @@
     for partner in partners:
         pl.semaphore_signal(barrier, inc=1, device_id=(partner,), device_id_type=MESH)
 
-    start, live = counts_of(counts, me)
+    start, live, cells = counts_of(counts, me)
     head = lax.rem(CHILD - lax.rem(start, CHILD), CHILD)
 
     def remote(source, to, send_sem, recv_sem, target):
@@ -227,9 +213,13 @@
     loads[0].wait()
 
     def transpose_primal(step, carry):
-        to_cell_major(p_t, primal, step)
+        to_cell_major(p_t, 0, primal, step)
         rows = pl.ds(pl.multiple_of(step * 96, 96), 96)
-        recon_hi[rows, :], recon_lo[rows, :] = split(recon[rows, :])
+        wide = jnp.concatenate([recon[rows, :], jnp.zeros((96, 768 - CHILD * DOF), F32)], 1)
+        hi, lo = split(wide)
+        recon3[rows, 0:768] = hi
+        recon3[rows, 768:1536] = hi
+        recon3[rows, 1536:2304] = lo
         return carry
 
     loads[1].wait()
@@ -240,14 +230,15 @@
     def send_primal(step, carry):
         k = lax.rem(step + FIRST_LIST, NEIGH)
         gather_list(picked, p_t, send, k)
-        to_cell_major(d_t, dual, step)
+        to_cell_major(padded, CHILD, dual, step)
         pack(p_out.at[k], picked)
         list_copy(p_out, p_in, p_send, p_recv, k).start()
         return carry
 
     lax.fori_loop(0, NEIGH, send_primal, 0)
-    first[...] = d_t[0:8, :]
-    last[...] = d_t[pl.ds(jnp.maximum(live, 8) - 8, 8), :]
+    first[...] = padded[8:16, :]
+    last[...] = padded[pl.ds(jnp.maximum(live, 8), 8), :]
+    padded[CELLS + 8 :, :] = jnp.zeros((padded.shape[0] - CELLS - 8, LANES), F32)
     edges = [remote(last, before, edge_send.at[0], edge_recv.at[0], behind(me, 1)),
              remote(first, after, edge_send.at[1], edge_recv.at[1], behind(me, -1))]
     for copy in edges:
@@ -256,6 +247,10 @@
     for i in range(3, len(staged)):
         loads[i].wait()
     fill_operator(operator, traction, trace)
+    hi, lo = split(operator[...].T)
+    operator3[0:256, :] = hi
+    operator3[256:512, :] = hi
+    operator3[512:768, :] = lo
     pair = (face_dir[...] // 2) * SLOTS
     index_a[...] = pair + face_cell[...]
     index_b[...] = pair + face_other[...]
@@ -269,16 +264,19 @@
         return carry
 
     lax.fori_loop(0, 8, residuals, 0)
+    for k in range(NEIGH):
+        onehot[:, k * GHOST : (k + 1) * GHOST] = low_onehot(send_v[k : k + 1, :])
     for copy in edges:
         copy.wait()
-    rebuild(head, live, d_t, before, after, recon_hi, recon_lo, w_t, padded, families, rebuilt, after2)
+    padded[0:8, :] = before[...]
+    rebuild(head, live, padded, after, after2, recon3, families, rebuilt, woven)
 
     def send_weight(step, carry):
         k = lax.rem(step + FIRST_LIST, NEIGH)
         at = pl.multiple_of(step * 256, 256)
-        gather_list(picked, w_t, send, k)
-        fill_table(table, at, p_t[pl.ds(at, 256), :], w_t[pl.ds(at, 256), :], operator)
-        cell_terms(term, load, w_t, cell_size, step)
+        gather_rows(picked, 0, woven, lambda i: send[k, i] + (CHILD - head), GHOST)
+        fill_table(table, at, p_t[pl.ds(at, 256), :], woven[pl.ds(CHILD - head + at, 256), :], operator3)
+        cell_terms(term, load, woven, CHILD - head, cell_size, step)
         pack(w_out.at[k], picked)
         list_copy(w_out, w_in, w_send, w_recv, k).start()
         return carry
@@ -293,7 +291,7 @@
         list_copy(w_out, w_in, w_send, w_recv, k).wait()
         row = step * 6
         gather_rows(side_a, row * LANES, table, lambda i: smem_a[row + i // LANES, i % LANES], 256)
-        fill_table(table, CELLS + k * GHOST, unpack(p_in[k]), unpack(w_in[k]), operator)
+        fill_table(table, CELLS + k * GHOST, unpack(p_in[k]), unpack(w_in[k]), operator3)
 
         def rest(r, carry):
             gather_rows(side_a, r * LANES, table, lambda i: smem_a[r, i], LANES)
@@ -326,8 +324,9 @@
         is_even = lanes_of(face_dir, c) % 2 == 0
         term_a = area * jnp.where(is_even, raw[1:2], raw[3:4])
         term_b = area * jnp.where(is_even, raw[0:1], raw[2:3])
-        sum_a += scatter(lanes_of(face_cell, c), term_a, CELLS // LANES)
-        sum_b += scatter(lanes_of(face_other, c), term_b, SLOTS // LANES)
+        cell, other = lanes_of(face_cell, c), lanes_of(face_other, c)
+        sum_a += scatter(cell, term_a, CELLS // LANES, low_onehot(cell))
+        sum_b += scatter(other, term_b, SLOTS // LANES, low_onehot(other))
         return sum_a, sum_b
 
     def body(i, carry):
@@ -344,41 +343,40 @@
     zero = (jnp.zeros((CELLS // LANES, LANES), F32), jnp.zeros((SLOTS // LANES, LANES), F32))
     raw, sums = lax.fori_loop(0, CHUNKS // 2, body, (jnp.zeros((8, CHUNK), F32), zero))
     sum_a, sum_b = add_sums(raw, CHUNKS - 1, sums)
-    backs = []
     for k in range(NEIGH):
         at = CELLS // LANES + 2 * k
-        partial[k, 0:2, :] = sum_b[at : at + 2]
-        backs.append(remote(partial.at[k], returned.at[k], b_send.at[k], b_recv.at[k], behind(me, -SHIFTS[k])))
-        backs[-1].start()
+        partial[k] = sum_b[at : at + 2]
+    backs = [remote(partial.at[k], returned.at[k], b_send, b_recv, behind(me, -SHIFTS[k])) for k in range(NEIGH)]
     for copy in backs:
-        copy.wait()
+        copy.start()
     index = jnp.concatenate([send_v[k : k + 1, :] for k in range(NEIGH)], 1)
+    out = term[...] + sum_a + sum_b[: CELLS // LANES]
+    remote(partial, returned, b_send, b_recv, behind(me, 1)).wait_recv()
     value = jnp.concatenate([returned[k, r : r + 1, :] for k in range(NEIGH) for r in range(2)], 1)
-    out = term[...] + sum_a + sum_b[: CELLS // LANES] + scatter(index, value, CELLS // LANES)
+    out = out + scatter(index, value, CELLS // LANES, onehot[...])
     slot = lax.broadcasted_iota(I32, out.shape, 0) * LANES + lax.broadcasted_iota(I32, out.shape, 1)
     indicator[...] = out
 
-    size = jnp.where(slot < live, jnp.abs(out), 0.0)
-    total = size[0:8] + size[8:16]
+    total = jnp.sum(jnp.where(slot < live, jnp.abs(out), 0.0), axis=0, keepdims=True)
     place = 0
     for stage, (stride, count) in enumerate(STAGES):
         part[stage] = total
-        copies = []
+        slots = pl.ds(place, count - 1)
         for step in range(1, count):
-            copies.append(remote(part.at[stage], parts.at[place + step - 1], r_send.at[place + step - 1],
-                                 r_recv.at[place + step - 1], in_stage(me, stride, count, step)))
-            copies[-1].start()
-        for step in range(1, count):
-            copies[step - 1].wait()
-            total += parts[place + step - 1]
+            remote(part.at[stage], parts.at[place + step - 1], r_send.at[stage], r_recv.at[stage],
+                   in_stage(me, stride, count, step)).start()
+        remote(parts.at[slots], parts.at[slots], r_send.at[stage], r_recv.at[stage], behind(me, 1)).wait_recv()
+        total = total + jnp.sum(parts[place : place + count - 1], axis=0)
         place += count - 1
 
-    def all_cells(i, carry):
-        return carry + counts[i]
-
-    cells = lax.fori_loop(0, RANKS, all_cells, jnp.int32(0), unroll=8)
     mean = jnp.sum(total) / cells.astype(F32)
     facts[...] = jnp.where(slot < live, mean, -1.0)
+    remote(partial, returned, b_send, b_recv, behind(me, 1)).wait_send()
+    place = 0
+    for stage, (stride, count) in enumerate(STAGES):
+        slots = pl.ds(place, count - 1)
+        remote(parts.at[slots], parts.at[slots], r_send.at[stage], r_recv.at[stage], behind(me, 1)).wait_send()
+        place += count - 1
 
 
 SMEM = pl.BlockSpec(memory_space=pltpu.SMEM)
@@ -391,6 +389,7 @@
     send = ghost_send[0]
     as_rows = lambda x: x.reshape(-1, LANES)
     f32 = lambda *shape: pltpu.VMEM(shape, F32)
+    bf16 = lambda *shape: pltpu.VMEM(shape, BF16)
     i32 = lambda *shape: pltpu.VMEM(shape, I32)
     dma = lambda n: pltpu.SemaphoreType.DMA((n,))
     rows = FACES // LANES
@@ -400,17 +399,17 @@
         f32(DOF, CELLS), f32(DOF, CELLS), f32(DOF, CELLS), f32(cells, LANES), i32(NEIGH, GHOST),
         i32(rows, LANES), i32(rows, LANES), i32(rows, LANES), i32(rows, LANES),
         f32(DOF, DOF), f32(768, CHILD * DOF), f32(6 * FACE_DOF, DOF), f32(6 * FACE_DOF, DOF),
-        f32(CELLS, LANES), f32(CELLS, LANES), f32(CELLS, LANES),
+        f32(CELLS, LANES),
         f32(8, LANES), f32(8, LANES), f32(8, LANES), f32(8, LANES), f32(16, LANES),
         f32(NEIGH, PACKED, LANES), f32(NEIGH, PACKED, LANES), f32(NEIGH, PACKED, LANES), f32(NEIGH, PACKED, LANES),
         f32(3 * THIRD, LANES),
-        f32(FAMILIES * CHILD + 8, LANES), f32(FAMILIES, 768), f32(FAMILIES, 768),
-        f32(384, 256), f32(3 * SLOTS, LANES), f32(FACES, LANES), f32(CHUNK, LANES), f32(CHUNK, LANES),
-        pltpu.VMEM((768, CHILD * DOF), BF16), pltpu.VMEM((768, CHILD * DOF), BF16),
+        f32(FAMILIES * CHILD + 8, LANES), f32(FAMILIES * CHILD, LANES), f32(FAMILIES, 768), f32(FAMILIES, 768),
+        f32(384, 256), bf16(768, 384), f32(3 * SLOTS, LANES), f32(FACES, LANES), f32(CHUNK, LANES), f32(CHUNK, LANES),
+        bf16(768, 2304), bf16(LANES, GHOSTS),
         i32(rows, LANES), i32(rows, LANES), pltpu.SMEM((rows, LANES), I32), pltpu.SMEM((rows, LANES), I32),
-        f32(cells, LANES), f32(NEIGH, 8, LANES), f32(NEIGH, 8, LANES), f32(len(STAGES), 8, LANES), f32(steps, 8, LANES),
-        dma(13), dma(2), dma(2), dma(2), dma(NEIGH), dma(NEIGH), dma(NEIGH), dma(NEIGH), dma(NEIGH), dma(NEIGH),
-        dma(steps), dma(steps),
+        f32(cells, LANES), f32(NEIGH, 2, LANES), f32(NEIGH, 2, LANES), f32(len(STAGES), 1, LANES), f32(steps, 1, LANES),
+        dma(13), dma(2), dma(2), dma(2), dma(NEIGH), dma(NEIGH), dma(NEIGH), dma(NEIGH),
+        pltpu.SemaphoreType.DMA, pltpu.SemaphoreType.DMA, dma(len(STAGES)), dma(len(STAGES)),
     ]
     indicator, facts = pl.pallas_call(
         kernel,

time: 63.9 us -> 62 us (0.970)
  Pallas kernels: 61.2 us -> 59.8 us
    pallas_call x1, Pallas kernels: 61.2 us -> 59.8 us  [per_device(): pl.pallas_call(kernel, out_shape=[jax.ShapeDtypeStruct((cells, LANES), F3...]
where the time goes in v4:
time: 62 us; the launch traced here: 61.8 us
  Pallas kernels  59.8 us (96%)
  other arithmetic  1.32 us (2%)
  between operations  0.64 us (1%)
    pallas_call x1, Pallas kernels, per_device(): pl.pallas_call(kernel, out_shape=[jax.ShapeDtypeStruct((cells, LANES), F3...  59.8 us
    div x1, other arithmetic, per_device(): return (indicator, jnp.abs(indicator) / (jnp.abs(facts) + 1e-06))  1.32 us

profile of v4, /device:TPU:0, one launch (start us, length us, event | category | flops | bytes accessed | tf_op | source)
XLA Modules:
  0.0 61.8 jit_solution(15352838676453595381)
XLA Ops:
  0.6 59.8 %indicators.1 = (f32[16,128]{1,0:T(8,128)}, f32[16,128]{1,0:T(8,128)}) custom-call(s32[128]{0:T(128)} %counts.1, s32[8,256]{1,0:T(8,128)} %bitcast.11, f32[81,2048]{1,0:T(8,128)} %primal_in.1, f32[81,2048]{1,0:T(8,128)} %dual_in.1, f32[81,2048]{1,0:T(8,128)} %load_in.1, f32[16,128]{1,0:T(8,128)} %bitcast.17, s32[8,256]{1,0:T(8,128)} %bitcast.12, ...), custom_call_target="tpu_custom_call" | custom-call | tf_op jit(solution)/shard_map/indicators/pallas_call | solution.py:414
  60.4 1.3 %bitcast_divide_fusion = (f32[2048]{0:T(1024)}, f32[2048]{0:T(1024)}) fusion(f32[16,128]{1,0:T(8,128)} %get-tuple-element.4, f32[16,128]{1,0:T(8,128)} %get-tuple-element.5), kind=kLoop, calls=%fused_computation | loop fusion | flops 12288 | bytes 32768 | tf_op jit(solution)/shard_map/div | solution.py:425

commit v5 on v4

--- a/solution.py
+++ b/solution.py
@@ -21,9 +21,9 @@
 SLOTS = CELLS + GHOSTS
 FACES = 6144
 LANES = 128
-LAG = 16
+BATCH = 16
 FAMILIES = 272
-THIRD = 88
+THIRD = 96
 PACKED = 2 * THIRD
 CHUNK = 256
 CHUNKS = FACES // CHUNK
@@ -43,38 +43,68 @@
     return lax.dot_general(a, b, (((1,), (0,)), ((), ())), preferred_element_type=F32)
 
 
-def gather_rows(dst, dst_at, src, index_of, count):
-    held = []
-    for i in range(count + LAG):
-        if i < count:
-            held.append(src[pl.ds(index_of(i), 1), :])
-        if i >= LAG:
-            dst[pl.ds(dst_at + (i - LAG), 1), :] = held[i - LAG]
-
-
-def turned_block(src, at):
-    return jnp.concatenate([src[:, pl.ds(at, 256)], jnp.zeros((LANES - DOF, 256), F32)], 0).T
-
-
-def to_cell_major(dst, row, src, step):
-    at = pl.multiple_of(step * 256, 256)
-    dst[pl.ds(pl.multiple_of(row + at, CHILD), 256), :] = turned_block(src, at)
-
-
-def pack(to, rows):
-    lane = lax.broadcasted_iota(I32, (THIRD, LANES), 1)
-    second = pltpu.roll(rows[THIRD : 2 * THIRD, :], DOF, 1)
-    third = pltpu.roll(rows[2 * THIRD :, :], 2 * DOF - LANES, 1)
-    upper = jnp.where(lane < DOF, rows[0:THIRD, :], second)
-    to[...] = jnp.concatenate([upper, jnp.where(lane < 2 * DOF - LANES, second, third)], 0)
-
-
-def unpack(rows):
-    lane = lax.broadcasted_iota(I32, (THIRD, LANES), 1)
-    upper, lower = rows[:THIRD], rows[THIRD:]
-    second = pltpu.roll(jnp.where(lane < 2 * DOF - LANES, lower, upper), LANES - DOF, 1)
-    third = pltpu.roll(lower, 2 * LANES - 2 * DOF, 1)
-    return jnp.concatenate([upper, second, third[: GHOST - PACKED]], 0)
+def gathers(dst, dst_at, src, index_of, count):
+    def step(base):
+        rows = [src[pl.ds(index_of(base + u), 1), :] for u in range(BATCH)]
+        for u in range(BATCH):
+            dst[pl.ds(dst_at + (base + u), 1), :] = rows[u]
+
+    return [functools.partial(step, base) for base in range(0, count, BATCH)]
+
+
+def together(*lists):
+    spread = [((i + 0.5) / len(steps), n, step) for n, steps in enumerate(lists) for i, step in enumerate(steps)]
+    for _, _, step in sorted(spread, key=lambda entry: entry[:2]):
+        step()
+
+
+def turns(dst, row, src, step):
+    def turn(half):
+        at = pl.multiple_of(step * 256 + half * LANES, LANES)
+        block = jnp.concatenate([src[:, pl.ds(at, LANES)], jnp.zeros((LANES - DOF, LANES), F32)], 0)
+        dst[pl.ds(pl.multiple_of(row + at, CHILD), LANES), :] = block.T
+
+    return [functools.partial(turn, half) for half in range(2)]
+
+
+def packs(to, rows):
+    lane = lax.broadcasted_iota(I32, (16, LANES), 1)
+
+    def step(at):
+        second = pltpu.roll(rows[THIRD + at : THIRD + at + 16, :], DOF, 1)
+        third = pltpu.roll(rows[2 * THIRD + at : 2 * THIRD + at + 16, :], 2 * DOF - LANES, 1)
+        to[at : at + 16, :] = jnp.where(lane < DOF, rows[at : at + 16, :], second)
+        to[THIRD + at : THIRD + at + 16, :] = jnp.where(lane < 2 * DOF - LANES, second, third)
+
+    return [functools.partial(step, at) for at in range(0, THIRD, 16)]
+
+
+def put_terms(x3, rows, lanes, value):
+    hi, lo = split(value)
+    x3[rows, lanes : lanes + LANES] = hi
+    x3[rows, 256 + lanes : 256 + lanes + LANES] = lo
+    x3[rows, 512 + lanes : 512 + lanes + LANES] = hi
+
+
+def unpacks(x3, lanes, rows):
+    lane = lax.broadcasted_iota(I32, (16, LANES), 1)
+
+    def step(at):
+        upper, lower = rows[at : at + 16, :], rows[THIRD + at : THIRD + at + 16, :]
+        second = pltpu.roll(jnp.where(lane < 2 * DOF - LANES, lower, upper), LANES - DOF, 1)
+        put_terms(x3, slice(at, at + 16), lanes, upper)
+        put_terms(x3, slice(THIRD + at, THIRD + at + 16), lanes, second)
+        if 2 * THIRD + at < GHOST:
+            put_terms(x3, slice(2 * THIRD + at, 2 * THIRD + at + 16), lanes, pltpu.roll(lower, 2 * LANES - 2 * DOF, 1))
+
+    return [functools.partial(step, at) for at in range(0, THIRD, 16)]
+
+
+def term_steps(x3, lanes, src, at):
+    def step(row):
+        put_terms(x3, slice(row, row + 32), lanes, src[pl.ds(at + row, 32), :])
+
+    return [functools.partial(step, row) for row in range(0, 256, 32)]
 
 
 def fill_operator(operator, traction, trace):
@@ -85,9 +115,8 @@
         operator[64 * d + 32 : 64 * d + 32 + FACE_DOF, LANES : LANES + DOF] = trace[rows, :]
 
 
-def fill_table(table, slot, p_rows, w_rows, operator):
-    hi, lo = split(jnp.concatenate([p_rows, w_rows], 1))
-    out = dot_nn(jnp.concatenate([hi, lo, hi], 1), operator[...])
+def fill_table(table, slot, x3, operator):
+    out = dot_nn(x3[...], operator[...])
     for pair in range(3):
         table[pl.ds(pl.multiple_of(pair * SLOTS + slot, 256), 256), :] = out[:, pair * LANES : (pair + 1) * LANES]
 
@@ -100,11 +129,14 @@
 
 
 def cell_terms(out, residual, woven, skip, cell_size, step):
-    cells = pl.ds(pl.multiple_of(step * 256, 256), 256)
-    total = jnp.sum(residual[:, cells] * woven[pl.ds(skip + step * 256, 256), :].T[:DOF, :], axis=0, keepdims=True)
-    for r in range(2):
-        i = step * 2 + r
-        out[pl.ds(i, 1), :] = cell_size[pl.ds(i, 1), :] * total[:, r * LANES : (r + 1) * LANES]
+    def half_step(half):
+        i = step * 2 + half
+        at = pl.multiple_of(i * LANES, LANES)
+        weight = woven[pl.ds(skip + at, LANES), :].T[:DOF, :]
+        total = jnp.sum(residual[:, pl.ds(at, LANES)] * weight, axis=0, keepdims=True)
+        out[pl.ds(i, 1), :] = cell_size[pl.ds(i, 1), :] * total
+
+    return [functools.partial(half_step, half) for half in range(2)]
 
 
 def lanes_of(ref, chunk):
@@ -153,35 +185,39 @@
     return me + (lax.rem(place + step, size) - place) * stride
 
 
-def gather_list(picked, source, send, k):
-    gather_rows(picked, 0, source, lambda i: send[k, i], GHOST)
-
-
-def rebuild(head, live, padded, after, after2, recon3, families, rebuilt, woven):
+def rebuild(head, live, padded, after, after2, recon3, families, f3, rebuilt, woven):
     after2[0:8, :] = jnp.zeros((8, LANES), F32)
     after2[8:16, :] = after[...]
     own = lax.rem(live - head + CHILD, CHILD)
     split_family = 1 + (live - head) // CHILD
-    row = lax.broadcasted_iota(I32, (FAMILIES, LANES), 0)
-    families[:, 640:768] = jnp.zeros((FAMILIES, LANES), F32)
-    for m in range(CHILD):
-        cells = padded[pl.ds(head + m, FAMILIES, stride=CHILD), :]
-        late = after2[pl.ds(CHILD + m - own, 1), :]
-        cells = jnp.where((row == split_family) & (m >= own), late, cells)
-        families[:, m * DOF : (m + 1) * DOF] = cells[:, :DOF]
-    hi, lo = split(families[...])
-    rebuilt[:, : CHILD * DOF] = dot_nt(jnp.concatenate([hi, lo, hi], 1), recon3[0 : CHILD * DOF, :])
-    lane = lax.broadcasted_iota(I32, (FAMILIES, LANES), 1)
-    for m in range(CHILD):
-        part = rebuilt[:, m * DOF : m * DOF + LANES]
-        woven[pl.ds(m, FAMILIES, stride=CHILD), :] = jnp.where(lane < DOF, part, 0.0)
+    for part in range(0, FAMILIES, 16):
+        row = part + lax.broadcasted_iota(I32, (16, LANES), 0)
+        rows = slice(part, part + 16)
+        families[rows, 640:768] = jnp.zeros((16, LANES), F32)
+        for m in range(CHILD):
+            cells = padded[pl.ds(head + m + part * CHILD, 16, stride=CHILD), :]
+            late = after2[pl.ds(CHILD + m - own, 1), :]
+            cells = jnp.where((row == split_family) & (m >= own), late, cells)
+            families[rows, m * DOF : (m + 1) * DOF] = cells[:, :DOF]
+        hi, lo = split(families[rows, :])
+        f3[rows, 0:768] = hi
+        f3[rows, 768:1536] = lo
+        f3[rows, 1536:2304] = hi
+    for part in range(0, CHILD * DOF, 256):
+        cols = slice(part, min(part + 256, CHILD * DOF))
+        rebuilt[:, cols] = dot_nt(f3[...], recon3[cols, :])
+    lane = lax.broadcasted_iota(I32, (16, LANES), 1)
+    for part in range(0, FAMILIES, 16):
+        for m in range(CHILD):
+            value = rebuilt[part : part + 16, m * DOF : m * DOF + LANES]
+            woven[pl.ds(m + part * CHILD, 16, stride=CHILD), :] = jnp.where(lane < DOF, value, 0.0)
 
 
 def kernel(counts, send, primal_in, dual_in, load_in, size_in, send_in, cell_in, other_in, dir_in, hanging_in,
            stiffness_in, recon_in, traction_in, trace_in,
            indicator, facts,
            primal, dual, load, cell_size, send_v, face_cell, face_other, face_dir, hanging, stiffness, recon, traction,
-           trace, p_t, first, last, before, after, after2, p_out, p_in, w_out, w_in, picked, padded, woven, families, rebuilt,
+           trace, p_t, first, last, before, after, after2, p_out, p_in, w_out, w_in, picked, packed, p_packed, padded, woven, families, f3, rebuilt, x3, mixed,
            operator, operator3, table, side_a, side_b0, side_b1, recon3, onehot, index_a, index_b, smem_a, smem_b, term, partial, returned, part, parts,
            in_sem, index_sem, edge_send, edge_recv, p_send, p_recv, w_send, w_recv, b_send, b_recv, r_send, r_recv):
     me = lax.axis_index("dom")
@@ -213,13 +249,14 @@
     loads[0].wait()
 
     def transpose_primal(step, carry):
-        to_cell_major(p_t, 0, primal, step)
-        rows = pl.ds(pl.multiple_of(step * 96, 96), 96)
-        wide = jnp.concatenate([recon[rows, :], jnp.zeros((96, 768 - CHILD * DOF), F32)], 1)
-        hi, lo = split(wide)
-        recon3[rows, 0:768] = hi
-        recon3[rows, 768:1536] = hi
-        recon3[rows, 1536:2304] = lo
+        def recon_step(part):
+            rows = pl.ds(pl.multiple_of(step * 96 + part * 16, 16), 16)
+            hi, lo = split(jnp.concatenate([recon[rows, :], jnp.zeros((16, 768 - CHILD * DOF), F32)], 1))
+            recon3[rows, 0:768] = hi
+            recon3[rows, 768:1536] = hi
+            recon3[rows, 1536:2304] = lo
+
+        together(turns(p_t, 0, primal, step), [functools.partial(recon_step, part) for part in range(6)])
         return carry
 
     loads[1].wait()
@@ -229,9 +266,9 @@
 
     def send_primal(step, carry):
         k = lax.rem(step + FIRST_LIST, NEIGH)
-        gather_list(picked, p_t, send, k)
-        to_cell_major(padded, CHILD, dual, step)
-        pack(p_out.at[k], picked)
+        together(gathers(picked, 0, p_t, lambda i: send[k, i], GHOST), turns(padded, CHILD, dual, step))
+        together(packs(packed, picked))
+        p_out[k] = packed[...]
         list_copy(p_out, p_in, p_send, p_recv, k).start()
         return carry
 
@@ -269,15 +306,18 @@
     for copy in edges:
         copy.wait()
     padded[0:8, :] = before[...]
-    rebuild(head, live, padded, after, after2, recon3, families, rebuilt, woven)
+    rebuild(head, live, padded, after, after2, recon3, families, f3, rebuilt, woven)
 
     def send_weight(step, carry):
         k = lax.rem(step + FIRST_LIST, NEIGH)
         at = pl.multiple_of(step * 256, 256)
-        gather_rows(picked, 0, woven, lambda i: send[k, i] + (CHILD - head), GHOST)
-        fill_table(table, at, p_t[pl.ds(at, 256), :], woven[pl.ds(CHILD - head + at, 256), :], operator3)
-        cell_terms(term, load, woven, CHILD - head, cell_size, step)
-        pack(w_out.at[k], picked)
+        skip = CHILD - head
+        terms = term_steps(x3, 0, p_t, at) + term_steps(x3, LANES, woven, skip + at)
+        table_step = functools.partial(fill_table, table, at, x3, operator3)
+        together(gathers(picked, 0, woven, lambda i: send[k, i] + skip, GHOST),
+                 terms + [table_step] + cell_terms(term, load, woven, skip, cell_size, step))
+        together(packs(packed, picked))
+        w_out[k] = packed[...]
         list_copy(w_out, w_in, w_send, w_recv, k).start()
         return carry
 
@@ -290,14 +330,19 @@
         list_copy(p_out, p_in, p_send, p_recv, k).wait()
         list_copy(w_out, w_in, w_send, w_recv, k).wait()
         row = step * 6
-        gather_rows(side_a, row * LANES, table, lambda i: smem_a[row + i // LANES, i % LANES], 256)
-        fill_table(table, CELLS + k * GHOST, unpack(p_in[k]), unpack(w_in[k]), operator3)
+        p_packed[...] = p_in[k]
+        packed[...] = w_in[k]
+        table_step = functools.partial(fill_table, table, CELLS + k * GHOST, x3, operator3)
+        together(gathers(side_a, row * LANES, table, lambda i: smem_a[row + i // LANES, i % LANES], 256),
+                 unpacks(x3, 0, p_packed) + unpacks(x3, LANES, packed))
+        together(gathers(side_a, row * LANES + 256, table, lambda i: smem_a[row + 2 + i // LANES, i % LANES], 256))
+        table_step()
 
         def rest(r, carry):
-            gather_rows(side_a, r * LANES, table, lambda i: smem_a[r, i], LANES)
+            together(gathers(side_a, r * LANES, table, lambda i: smem_a[r, i], LANES))
             return carry
 
-        lax.fori_loop(row + 2, row + 6, rest, 0)
+        lax.fori_loop(row + 4, row + 6, rest, 0)
         return carry
 
     lax.fori_loop(0, NEIGH, take_ghosts, 0)
@@ -305,17 +350,23 @@
     lane = lax.broadcasted_iota(I32, (8, 2 * LANES), 1) % LANES
     sub = lax.broadcasted_iota(I32, (8, 2 * LANES), 0)
     pick = jnp.where(lane // 32 == sub, 1.0, 0.0).astype(BF16)
-    upper = lax.broadcasted_iota(I32, (CHUNK, LANES), 1) % 64 >= 32
+    upper = lax.broadcasted_iota(I32, (16, LANES), 1) % 64 >= 32
 
     def gather_b(to, c):
-        gather_rows(to, 0, table, lambda i: smem_b[c * SPLIT + i // LANES, i % LANES], CHUNK)
-
-    def raw_sums(side_b, c):
-        a = side_a[pl.ds(pl.multiple_of(c * CHUNK, CHUNK), CHUNK), :]
-        b = pltpu.roll(side_b[...], 64, 1)
-        jump = pltpu.roll(a + b, 32, 1)
-        hi, lo = split(jnp.where(upper, jump * a, pltpu.roll(jump * b, 96, 1)))
-        return dot_nt(pick, jnp.concatenate([hi, lo], 1))
+        return gathers(to, 0, table, lambda i: smem_b[c * SPLIT + i // LANES, i % LANES], CHUNK)
+
+    def mix_steps(side_b, c):
+        def step(row):
+            a = side_a[pl.ds(pl.multiple_of(c * CHUNK + row, 16), 16), :]
+            b = pltpu.roll(side_b[row : row + 16, :], 64, 1)
+            jump = pltpu.roll(a + b, 32, 1)
+            hi, lo = split(jnp.where(upper, jump * a, pltpu.roll(jump * b, 96, 1)))
+            mixed[row : row + 16, :] = jnp.concatenate([hi, lo], 1)
+
+        return [functools.partial(step, row) for row in range(0, CHUNK, 16)]
+
+    def raw_sums():
+        return dot_nt(pick, mixed[...])
 
     def add_sums(raw, c, carry):
         sum_a, sum_b = carry
@@ -331,15 +382,15 @@
 
     def body(i, carry):
         raw_before, sums = carry
-        gather_b(side_b1, 2 * i + 1)
-        raw = raw_sums(side_b0, 2 * i)
+        together(gather_b(side_b1, 2 * i + 1), mix_steps(side_b0, 2 * i))
+        raw = raw_sums()
         sums = add_sums(raw_before, jnp.maximum(2 * i - 1, 0), sums)
-        gather_b(side_b0, jnp.minimum(2 * i + 2, CHUNKS - 1))
-        raw_after = raw_sums(side_b1, 2 * i + 1)
+        together(gather_b(side_b0, jnp.minimum(2 * i + 2, CHUNKS - 1)), mix_steps(side_b1, 2 * i + 1))
+        raw_after = raw_sums()
         sums = add_sums(raw, 2 * i, sums)
         return raw_after, sums
 
-    gather_b(side_b0, 0)
+    together(gather_b(side_b0, 0))
     zero = (jnp.zeros((CELLS // LANES, LANES), F32), jnp.zeros((SLOTS // LANES, LANES), F32))
     raw, sums = lax.fori_loop(0, CHUNKS // 2, body, (jnp.zeros((8, CHUNK), F32), zero))
     sum_a, sum_b = add_sums(raw, CHUNKS - 1, sums)
@@ -402,8 +453,9 @@
         f32(CELLS, LANES),
         f32(8, LANES), f32(8, LANES), f32(8, LANES), f32(8, LANES), f32(16, LANES),
         f32(NEIGH, PACKED, LANES), f32(NEIGH, PACKED, LANES), f32(NEIGH, PACKED, LANES), f32(NEIGH, PACKED, LANES),
-        f32(3 * THIRD, LANES),
-        f32(FAMILIES * CHILD + 8, LANES), f32(FAMILIES * CHILD, LANES), f32(FAMILIES, 768), f32(FAMILIES, 768),
+        f32(3 * THIRD, LANES), f32(PACKED, LANES), f32(PACKED, LANES),
+        f32(FAMILIES * CHILD + 8, LANES), f32(FAMILIES * CHILD, LANES), f32(FAMILIES, 768), bf16(FAMILIES, 2304), f32(FAMILIES, 768),
+        bf16(256, 768), bf16(CHUNK, 2 * LANES),
         f32(384, 256), bf16(768, 384), f32(3 * SLOTS, LANES), f32(FACES, LANES), f32(CHUNK, LANES), f32(CHUNK, LANES),
         bf16(768, 2304), bf16(LANES, GHOSTS),
         i32(rows, LANES), i32(rows, LANES), pltpu.SMEM((rows, LANES), I32), pltpu.SMEM((rows, LANES), I32),

time: 62 us -> 64.1 us (1.034)
  Pallas kernels: 59.8 us -> 61.9 us
    pallas_call x1, Pallas kernels: 59.8 us -> 61.9 us  [per_device(): pl.pallas_call(kernel, out_shape=[jax.ShapeDtypeStruct((cells, LANES), F3...]
where the time goes in v5:
time: 64.1 us; the launch traced here: 63.9 us
  Pallas kernels  61.9 us (97%)
  other arithmetic  1.32 us (2%)
    pallas_call x1, Pallas kernels, per_device(): pl.pallas_call(kernel, out_shape=[jax.ShapeDtypeStruct((cells, LANES), F3...  61.9 us
    div x1, other arithmetic, per_device(): return (indicator, jnp.abs(indicator) / (jnp.abs(facts) + 1e-06))  1.32 us

profile of v5, /device:TPU:0, one launch (start us, length us, event | category | flops | bytes accessed | tf_op | source)
XLA Modules:
  0.0 63.9 jit_solution(8734266608022462507)
XLA Ops:
  0.6 61.9 %indicators.1 = (f32[16,128]{1,0:T(8,128)}, f32[16,128]{1,0:T(8,128)}) custom-call(s32[128]{0:T(128)} %counts.1, s32[8,256]{1,0:T(8,128)} %bitcast.11, f32[81,2048]{1,0:T(8,128)} %primal_in.1, f32[81,2048]{1,0:T(8,128)} %dual_in.1, f32[81,2048]{1,0:T(8,128)} %load_in.1, f32[16,128]{1,0:T(8,128)} %bitcast.17, s32[8,256]{1,0:T(8,128)} %bitcast.12, ...), custom_call_target="tpu_custom_call" | custom-call | tf_op jit(solution)/shard_map/indicators/pallas_call | solution.py:466
  62.5 1.3 %bitcast_divide_fusion = (f32[2048]{0:T(1024)}, f32[2048]{0:T(1024)}) fusion(f32[16,128]{1,0:T(8,128)} %get-tuple-element.4, f32[16,128]{1,0:T(8,128)} %get-tuple-element.5), kind=kLoop, calls=%fused_computation | loop fusion | flops 12288 | bytes 32768 | tf_op jit(solution)/shard_map/div | solution.py:477

commit v6 on v4

--- a/solution.py
+++ b/solution.py
@@ -21,7 +21,6 @@
 SLOTS = CELLS + GHOSTS
 FACES = 6144
 LANES = 128
-LAG = 16
 FAMILIES = 272
 THIRD = 88
 PACKED = 2 * THIRD
@@ -44,12 +43,13 @@
 
 
 def gather_rows(dst, dst_at, src, index_of, count):
-    held = []
-    for i in range(count + LAG):
-        if i < count:
-            held.append(src[pl.ds(index_of(i), 1), :])
-        if i >= LAG:
-            dst[pl.ds(dst_at + (i - LAG), 1), :] = held[i - LAG]
+    sub = lax.broadcasted_iota(I32, (8, LANES), 0)
+    for base in range(0, count, 8):
+        rows = [src[pl.ds(index_of(base + u), 1), :] for u in range(8)]
+        tile = jnp.broadcast_to(rows[0], (8, LANES))
+        for u in range(1, 8):
+            tile = jnp.where(sub == u, jnp.broadcast_to(rows[u], (8, LANES)), tile)
+        dst[pl.ds(pl.multiple_of(dst_at + base, 8), 8), :] = tile
 
 
 def turned_block(src, at):

time: 62 us -> 61.9 us (level)
  no operation moved by 1% of the time
where the time goes in v6:
time: 61.9 us; the launch traced here: 61.7 us
  Pallas kernels  59.7 us (96%)
  other arithmetic  1.32 us (2%)
  between operations  0.64 us (1%)
    pallas_call x1, Pallas kernels, per_device(): pl.pallas_call(kernel, out_shape=[jax.ShapeDtypeStruct((cells, LANES), F3...  59.7 us
    div x1, other arithmetic, per_device(): return (indicator, jnp.abs(indicator) / (jnp.abs(facts) + 1e-06))  1.32 us

profile of v6, /device:TPU:0, one launch (start us, length us, event | category | flops | bytes accessed | tf_op | source)
XLA Modules:
  0.0 61.7 jit_solution(14354789433767538909)
XLA Ops:
  0.6 59.7 %indicators.1 = (f32[16,128]{1,0:T(8,128)}, f32[16,128]{1,0:T(8,128)}) custom-call(s32[128]{0:T(128)} %counts.1, s32[8,256]{1,0:T(8,128)} %bitcast.11, f32[81,2048]{1,0:T(8,128)} %primal_in.1, f32[81,2048]{1,0:T(8,128)} %dual_in.1, f32[81,2048]{1,0:T(8,128)} %load_in.1, f32[16,128]{1,0:T(8,128)} %bitcast.17, s32[8,256]{1,0:T(8,128)} %bitcast.12, ...), custom_call_target="tpu_custom_call" | custom-call | tf_op jit(solution)/shard_map/indicators/pallas_call | solution.py:414
  60.3 1.3 %bitcast_divide_fusion = (f32[2048]{0:T(1024)}, f32[2048]{0:T(1024)}) fusion(f32[16,128]{1,0:T(8,128)} %get-tuple-element.4, f32[16,128]{1,0:T(8,128)} %get-tuple-element.5), kind=kLoop, calls=%fused_computation | loop fusion | flops 12288 | bytes 32768 | tf_op jit(solution)/shard_map/div | solution.py:425

commit v7 on v6

--- a/solution.py
+++ b/solution.py
@@ -185,7 +185,7 @@
            operator, operator3, table, side_a, side_b0, side_b1, recon3, onehot, index_a, index_b, smem_a, smem_b, term, partial, returned, part, parts,
            in_sem, index_sem, edge_send, edge_recv, p_send, p_recv, w_send, w_recv, b_send, b_recv, r_send, r_recv):
     me = lax.axis_index("dom")
-    staged = [(primal_in, primal), (recon_in, recon.at[pl.ds(0, CHILD * DOF), :]), (dual_in, dual), (traction_in, traction), (trace_in, trace),
+    staged = [(dual_in, dual), (primal_in, primal), (recon_in, recon.at[pl.ds(0, CHILD * DOF), :]), (traction_in, traction), (trace_in, trace),
               (load_in, load), (size_in, cell_size), (stiffness_in, stiffness), (cell_in, face_cell),
               (other_in, face_other), (dir_in, face_dir), (hanging_in, hanging), (send_in, send_v)]
     loads = {}
@@ -211,6 +211,23 @@
         return remote(source.at[k], to.at[k], send_sem.at[k], recv_sem.at[k], behind(me, shift_of(k)))
 
     loads[0].wait()
+    cell = lax.broadcasted_iota(I32, (16, CELLS), 1)
+    row = lax.broadcasted_iota(I32, (16, CELLS), 0)
+    picked_cell = jnp.where(row < CHILD, row, live - 2 * CHILD + row)
+    chosen = jnp.where(cell == picked_cell, 1.0, 0.0).astype(BF16)
+    hi, lo = split(dual[...])
+    ends = dot_nt(chosen, hi) + dot_nt(chosen, lo)
+    first[...] = jnp.zeros((8, LANES), F32)
+    last[...] = jnp.zeros((8, LANES), F32)
+    first[:, :DOF] = ends[:CHILD]
+    last[:, :DOF] = ends[CHILD:]
+    pl.semaphore_wait(barrier, len(partners))
+    edges = [remote(last, before, edge_send.at[0], edge_recv.at[0], behind(me, 1)),
+             remote(first, after, edge_send.at[1], edge_recv.at[1], behind(me, -1))]
+    for copy in edges:
+        copy.start()
+
+    loads[1].wait()
 
     def transpose_primal(step, carry):
         to_cell_major(p_t, 0, primal, step)
@@ -222,10 +239,8 @@
         recon3[rows, 1536:2304] = lo
         return carry
 
-    loads[1].wait()
+    loads[2].wait()
     lax.fori_loop(0, 8, transpose_primal, 0)
-    loads[2].wait()
-    pl.semaphore_wait(barrier, len(partners))
 
     def send_primal(step, carry):
         k = lax.rem(step + FIRST_LIST, NEIGH)
@@ -236,14 +251,7 @@
         return carry
 
     lax.fori_loop(0, NEIGH, send_primal, 0)
-    first[...] = padded[8:16, :]
-    last[...] = padded[pl.ds(jnp.maximum(live, 8), 8), :]
     padded[CELLS + 8 :, :] = jnp.zeros((padded.shape[0] - CELLS - 8, LANES), F32)
-    edges = [remote(last, before, edge_send.at[0], edge_recv.at[0], behind(me, 1)),
-             remote(first, after, edge_send.at[1], edge_recv.at[1], behind(me, -1))]
-    for copy in edges:
-        copy.start()
-
     for i in range(3, len(staged)):
         loads[i].wait()
     fill_operator(operator, traction, trace)

time: 61.9 us -> 57.6 us (0.931)
  Pallas kernels: 59.7 us -> 55.4 us
    pallas_call x1, Pallas kernels: 59.7 us -> 55.4 us  [per_device(): pl.pallas_call(kernel, out_shape=[jax.ShapeDtypeStruct((cells, LANES), F3...]
where the time goes in v7:
time: 57.6 us; the launch traced here: 57.4 us
  Pallas kernels  55.4 us (96%)
  other arithmetic  1.32 us (2%)
  between operations  0.64 us (1%)
    pallas_call x1, Pallas kernels, per_device(): pl.pallas_call(kernel, out_shape=[jax.ShapeDtypeStruct((cells, LANES), F3...  55.4 us
    div x1, other arithmetic, per_device(): return (indicator, jnp.abs(indicator) / (jnp.abs(facts) + 1e-06))  1.32 us

profile of v7, /device:TPU:0, one launch (start us, length us, event | category | flops | bytes accessed | tf_op | source)
XLA Modules:
  0.0 57.4 jit_solution(176076312093286337)
XLA Ops:
  0.6 55.4 %indicators.1 = (f32[16,128]{1,0:T(8,128)}, f32[16,128]{1,0:T(8,128)}) custom-call(s32[128]{0:T(128)} %counts.1, s32[8,256]{1,0:T(8,128)} %bitcast.11, f32[81,2048]{1,0:T(8,128)} %primal_in.1, f32[81,2048]{1,0:T(8,128)} %dual_in.1, f32[81,2048]{1,0:T(8,128)} %load_in.1, f32[16,128]{1,0:T(8,128)} %bitcast.17, s32[8,256]{1,0:T(8,128)} %bitcast.12, ...), custom_call_target="tpu_custom_call" | custom-call | tf_op jit(solution)/shard_map/indicators/pallas_call | solution.py:422
  56.1 1.3 %bitcast_divide_fusion = (f32[2048]{0:T(1024)}, f32[2048]{0:T(1024)}) fusion(f32[16,128]{1,0:T(8,128)} %get-tuple-element.4, f32[16,128]{1,0:T(8,128)} %get-tuple-element.5), kind=kLoop, calls=%fused_computation | loop fusion | flops 12288 | bytes 32768 | tf_op jit(solution)/shard_map/div | solution.py:433

commit v8 on v7

--- a/solution.py
+++ b/solution.py
@@ -126,6 +126,7 @@
 RANKS = 128
 SHIFTS = [(1 << which // 2) * (1 - 2 * (which % 2)) for which in range(NEIGH)]
 FIRST_LIST = 4
+SEND_ORDER = [4, 5, 6, 7, 2, 3, 0, 1]
 STAGES = ((1, 8), (8, 16))
 
 
@@ -242,16 +243,6 @@
     loads[2].wait()
     lax.fori_loop(0, 8, transpose_primal, 0)
 
-    def send_primal(step, carry):
-        k = lax.rem(step + FIRST_LIST, NEIGH)
-        gather_list(picked, p_t, send, k)
-        to_cell_major(padded, CHILD, dual, step)
-        pack(p_out.at[k], picked)
-        list_copy(p_out, p_in, p_send, p_recv, k).start()
-        return carry
-
-    lax.fori_loop(0, NEIGH, send_primal, 0)
-    padded[CELLS + 8 :, :] = jnp.zeros((padded.shape[0] - CELLS - 8, LANES), F32)
     for i in range(3, len(staged)):
         loads[i].wait()
     fill_operator(operator, traction, trace)
@@ -267,13 +258,18 @@
     copy_a.start()
     copy_b.start()
 
-    def residuals(step, carry):
+    def send_primal(step, carry):
+        k = lax.rem(step + FIRST_LIST, NEIGH)
+        gather_list(picked, p_t, send, k)
+        to_cell_major(padded, CHILD, dual, step)
         take_residual(load, primal, stiffness, step)
+        onehot[:, pl.ds(pl.multiple_of(step * GHOST, GHOST), GHOST)] = low_onehot(send_v[pl.ds(step, 1), :])
+        pack(p_out.at[k], picked)
+        list_copy(p_out, p_in, p_send, p_recv, k).start()
         return carry
 
-    lax.fori_loop(0, 8, residuals, 0)
-    for k in range(NEIGH):
-        onehot[:, k * GHOST : (k + 1) * GHOST] = low_onehot(send_v[k : k + 1, :])
+    lax.fori_loop(0, NEIGH, send_primal, 0)
+    padded[CELLS + 8 :, :] = jnp.zeros((padded.shape[0] - CELLS - 8, LANES), F32)
     for copy in edges:
         copy.wait()
     padded[0:8, :] = before[...]
@@ -298,14 +294,14 @@
         list_copy(p_out, p_in, p_send, p_recv, k).wait()
         list_copy(w_out, w_in, w_send, w_recv, k).wait()
         row = step * 6
-        gather_rows(side_a, row * LANES, table, lambda i: smem_a[row + i // LANES, i % LANES], 256)
+        gather_rows(side_a, row * LANES, table, lambda i: smem_a[row + i // LANES, i % LANES], 512)
         fill_table(table, CELLS + k * GHOST, unpack(p_in[k]), unpack(w_in[k]), operator3)
 
         def rest(r, carry):
             gather_rows(side_a, r * LANES, table, lambda i: smem_a[r, i], LANES)
             return carry
 
-        lax.fori_loop(row + 2, row + 6, rest, 0)
+        lax.fori_loop(row + 4, row + 6, rest, 0)
         return carry
 
     lax.fori_loop(0, NEIGH, take_ghosts, 0)
@@ -351,10 +347,10 @@
     zero = (jnp.zeros((CELLS // LANES, LANES), F32), jnp.zeros((SLOTS // LANES, LANES), F32))
     raw, sums = lax.fori_loop(0, CHUNKS // 2, body, (jnp.zeros((8, CHUNK), F32), zero))
     sum_a, sum_b = add_sums(raw, CHUNKS - 1, sums)
-    for k in range(NEIGH):
+    for k in SEND_ORDER:
         at = CELLS // LANES + 2 * k
         partial[k] = sum_b[at : at + 2]
-    backs = [remote(partial.at[k], returned.at[k], b_send, b_recv, behind(me, -SHIFTS[k])) for k in range(NEIGH)]
+    backs = [remote(partial.at[k], returned.at[k], b_send, b_recv, behind(me, -SHIFTS[k])) for k in SEND_ORDER]
     for copy in backs:
         copy.start()
     index = jnp.concatenate([send_v[k : k + 1, :] for k in range(NEIGH)], 1)

time: 57.6 us -> 58.8 us (1.021)
  Pallas kernels: 55.4 us -> 56.6 us
    pallas_call x1, Pallas kernels: 55.4 us -> 56.6 us  [per_device(): pl.pallas_call(kernel, out_shape=[jax.ShapeDtypeStruct((cells, LANES), F3...]
where the time goes in v8:
time: 58.8 us; the launch traced here: 58.6 us
  Pallas kernels  56.6 us (96%)
  other arithmetic  1.32 us (2%)
  between operations  0.64 us (1%)
    pallas_call x1, Pallas kernels, per_device(): pl.pallas_call(kernel, out_shape=[jax.ShapeDtypeStruct((cells, LANES), F3...  56.6 us
    div x1, other arithmetic, per_device(): return (indicator, jnp.abs(indicator) / (jnp.abs(facts) + 1e-06))  1.32 us

profile of v8, /device:TPU:0, one launch (start us, length us, event | category | flops | bytes accessed | tf_op | source)
XLA Modules:
  0.0 58.6 jit_solution(13769118106846874936)
XLA Ops:
  0.6 56.6 %indicators.1 = (f32[16,128]{1,0:T(8,128)}, f32[16,128]{1,0:T(8,128)}) custom-call(s32[128]{0:T(128)} %counts.1, s32[8,256]{1,0:T(8,128)} %bitcast.11, f32[81,2048]{1,0:T(8,128)} %primal_in.1, f32[81,2048]{1,0:T(8,128)} %dual_in.1, f32[81,2048]{1,0:T(8,128)} %load_in.1, f32[16,128]{1,0:T(8,128)} %bitcast.17, s32[8,256]{1,0:T(8,128)} %bitcast.12, ...), custom_call_target="tpu_custom_call" | custom-call | tf_op jit(solution)/shard_map/indicators/pallas_call | solution.py:418
  57.3 1.3 %bitcast_divide_fusion = (f32[2048]{0:T(1024)}, f32[2048]{0:T(1024)}) fusion(f32[16,128]{1,0:T(8,128)} %get-tuple-element.4, f32[16,128]{1,0:T(8,128)} %get-tuple-element.5), kind=kLoop, calls=%fused_computation | loop fusion | flops 12288 | bytes 32768 | tf_op jit(solution)/shard_map/div | solution.py:429

commit v9 on v7

--- a/solution.py
+++ b/solution.py
@@ -126,6 +126,7 @@
 RANKS = 128
 SHIFTS = [(1 << which // 2) * (1 - 2 * (which % 2)) for which in range(NEIGH)]
 FIRST_LIST = 4
+SEND_ORDER = [4, 5, 6, 7, 2, 3, 0, 1]
 STAGES = ((1, 8), (8, 16))
 
 
@@ -185,7 +186,7 @@
            operator, operator3, table, side_a, side_b0, side_b1, recon3, onehot, index_a, index_b, smem_a, smem_b, term, partial, returned, part, parts,
            in_sem, index_sem, edge_send, edge_recv, p_send, p_recv, w_send, w_recv, b_send, b_recv, r_send, r_recv):
     me = lax.axis_index("dom")
-    staged = [(dual_in, dual), (primal_in, primal), (recon_in, recon.at[pl.ds(0, CHILD * DOF), :]), (traction_in, traction), (trace_in, trace),
+    staged = [(primal_in, primal), (dual_in, dual), (recon_in, recon.at[pl.ds(0, CHILD * DOF), :]), (traction_in, traction), (trace_in, trace),
               (load_in, load), (size_in, cell_size), (stiffness_in, stiffness), (cell_in, face_cell),
               (other_in, face_other), (dir_in, face_dir), (hanging_in, hanging), (send_in, send_v)]
     loads = {}
@@ -210,7 +211,13 @@
     def list_copy(source, to, send_sem, recv_sem, k):
         return remote(source.at[k], to.at[k], send_sem.at[k], recv_sem.at[k], behind(me, shift_of(k)))
 
+    def transpose_primal(step, carry):
+        to_cell_major(p_t, 0, primal, step)
+        return carry
+
     loads[0].wait()
+    lax.fori_loop(0, 8, transpose_primal, 0)
+    loads[1].wait()
     cell = lax.broadcasted_iota(I32, (16, CELLS), 1)
     row = lax.broadcasted_iota(I32, (16, CELLS), 0)
     picked_cell = jnp.where(row < CHILD, row, live - 2 * CHILD + row)
@@ -227,10 +234,18 @@
     for copy in edges:
         copy.start()
 
-    loads[1].wait()
-
-    def transpose_primal(step, carry):
-        to_cell_major(p_t, 0, primal, step)
+    def send_primal(step, carry):
+        k = lax.rem(step + FIRST_LIST, NEIGH)
+        gather_list(picked, p_t, send, k)
+        to_cell_major(padded, CHILD, dual, step)
+        pack(p_out.at[k], picked)
+        list_copy(p_out, p_in, p_send, p_recv, k).start()
+        return carry
+
+    lax.fori_loop(0, NEIGH, send_primal, 0)
+    padded[CELLS + 8 :, :] = jnp.zeros((padded.shape[0] - CELLS - 8, LANES), F32)
+
+    def split_recon(step, carry):
         rows = pl.ds(pl.multiple_of(step * 96, 96), 96)
         wide = jnp.concatenate([recon[rows, :], jnp.zeros((96, 768 - CHILD * DOF), F32)], 1)
         hi, lo = split(wide)
@@ -240,18 +255,7 @@
         return carry
 
     loads[2].wait()
-    lax.fori_loop(0, 8, transpose_primal, 0)
-
-    def send_primal(step, carry):
-        k = lax.rem(step + FIRST_LIST, NEIGH)
-        gather_list(picked, p_t, send, k)
-        to_cell_major(padded, CHILD, dual, step)
-        pack(p_out.at[k], picked)
-        list_copy(p_out, p_in, p_send, p_recv, k).start()
-        return carry
-
-    lax.fori_loop(0, NEIGH, send_primal, 0)
-    padded[CELLS + 8 :, :] = jnp.zeros((padded.shape[0] - CELLS - 8, LANES), F32)
+    lax.fori_loop(0, 7, split_recon, 0)
     for i in range(3, len(staged)):
         loads[i].wait()
     fill_operator(operator, traction, trace)
@@ -351,10 +355,10 @@
     zero = (jnp.zeros((CELLS // LANES, LANES), F32), jnp.zeros((SLOTS // LANES, LANES), F32))
     raw, sums = lax.fori_loop(0, CHUNKS // 2, body, (jnp.zeros((8, CHUNK), F32), zero))
     sum_a, sum_b = add_sums(raw, CHUNKS - 1, sums)
-    for k in range(NEIGH):
+    for k in SEND_ORDER:
         at = CELLS // LANES + 2 * k
         partial[k] = sum_b[at : at + 2]
-    backs = [remote(partial.at[k], returned.at[k], b_send, b_recv, behind(me, -SHIFTS[k])) for k in range(NEIGH)]
+    backs = [remote(partial.at[k], returned.at[k], b_send, b_recv, behind(me, -SHIFTS[k])) for k in SEND_ORDER]
     for copy in backs:
         copy.start()
     index = jnp.concatenate([send_v[k : k + 1, :] for k in range(NEIGH)], 1)

time: 57.6 us -> 56.8 us (0.986)
  Pallas kernels: 55.4 us -> 54.6 us
    pallas_call x1, Pallas kernels: 55.4 us -> 54.6 us  [per_device(): pl.pallas_call(kernel, out_shape=[jax.ShapeDtypeStruct((cells, LANES), F3...]
where the time goes in v9:
time: 56.8 us; the launch traced here: 56.6 us
  Pallas kernels  54.6 us (96%)
  other arithmetic  1.32 us (2%)
  between operations  0.64 us (1%)
    pallas_call x1, Pallas kernels, per_device(): pl.pallas_call(kernel, out_shape=[jax.ShapeDtypeStruct((cells, LANES), F3...  54.6 us
    div x1, other arithmetic, per_device(): return (indicator, jnp.abs(indicator) / (jnp.abs(facts) + 1e-06))  1.32 us

profile of v9, /device:TPU:0, one launch (start us, length us, event | category | flops | bytes accessed | tf_op | source)
XLA Modules:
  0.0 56.6 jit_solution(11022823356561627600)
XLA Ops:
  0.6 54.6 %indicators.1 = (f32[16,128]{1,0:T(8,128)}, f32[16,128]{1,0:T(8,128)}) custom-call(s32[128]{0:T(128)} %counts.1, s32[8,256]{1,0:T(8,128)} %bitcast.11, f32[81,2048]{1,0:T(8,128)} %primal_in.1, f32[81,2048]{1,0:T(8,128)} %dual_in.1, f32[81,2048]{1,0:T(8,128)} %load_in.1, f32[16,128]{1,0:T(8,128)} %bitcast.17, s32[8,256]{1,0:T(8,128)} %bitcast.12, ...), custom_call_target="tpu_custom_call" | custom-call | tf_op jit(solution)/shard_map/indicators/pallas_call | solution.py:426
  55.2 1.3 %bitcast_divide_fusion = (f32[2048]{0:T(1024)}, f32[2048]{0:T(1024)}) fusion(f32[16,128]{1,0:T(8,128)} %get-tuple-element.4, f32[16,128]{1,0:T(8,128)} %get-tuple-element.5), kind=kLoop, calls=%fused_computation | loop fusion | flops 12288 | bytes 32768 | tf_op jit(solution)/shard_map/div | solution.py:437

commit v10 on v9

--- a/solution.py
+++ b/solution.py
@@ -69,6 +69,14 @@
     to[...] = jnp.concatenate([upper, jnp.where(lane < 2 * DOF - LANES, second, third)], 0)
 
 
+def pack_halves(to, j, rows):
+    lane = lax.broadcasted_iota(I32, (THIRD, LANES), 1)
+    second = pltpu.roll(rows[THIRD : 2 * THIRD, :], DOF, 1)
+    third = pltpu.roll(rows[2 * THIRD :, :], 2 * DOF - LANES, 1)
+    to[j, 0] = jnp.where(lane < DOF, rows[0:THIRD, :], second)
+    to[j, 1] = jnp.where(lane < 2 * DOF - LANES, second, third)
+
+
 def unpack(rows):
     lane = lax.broadcasted_iota(I32, (THIRD, LANES), 1)
     upper, lower = rows[:THIRD], rows[THIRD:]
@@ -126,6 +134,7 @@
 RANKS = 128
 SHIFTS = [(1 << which // 2) * (1 - 2 * (which % 2)) for which in range(NEIGH)]
 FIRST_LIST = 4
+FAR = (4, 5)
 SEND_ORDER = [4, 5, 6, 7, 2, 3, 0, 1]
 STAGES = ((1, 8), (8, 16))
 
@@ -141,6 +150,10 @@
 
 def behind(me, by):
     return lax.rem(me + (by + RANKS), RANKS)
+
+
+def beside(me, way):
+    return in_stage(me, 2, 4, 1 + 2 * way)
 
 
 def shift_of(k):
@@ -182,7 +195,7 @@
            stiffness_in, recon_in, traction_in, trace_in,
            indicator, facts,
            primal, dual, load, cell_size, send_v, face_cell, face_other, face_dir, hanging, stiffness, recon, traction,
-           trace, p_t, first, last, before, after, after2, p_out, p_in, w_out, w_in, picked, padded, woven, families, rebuilt,
+           trace, p_t, first, last, before, after, after2, p_out, p_in, w_out, w_in, far_p, far_p_mid, far_p_in, far_w, far_w_mid, far_w_in, far_sem, picked, padded, woven, families, rebuilt,
            operator, operator3, table, side_a, side_b0, side_b1, recon3, onehot, index_a, index_b, smem_a, smem_b, term, partial, returned, part, parts,
            in_sem, index_sem, edge_send, edge_recv, p_send, p_recv, w_send, w_recv, b_send, b_recv, r_send, r_recv):
     me = lax.axis_index("dom")
@@ -196,6 +209,7 @@
 
     barrier = pltpu.get_barrier_semaphore()
     partners = [behind(me, shift) for shift in SHIFTS]
+    partners += [beside(behind(me, -SHIFTS[k]), way) for k in FAR for way in range(2)]
     for stride, size in STAGES:
         partners += [in_stage(me, stride, size, step) for step in range(1, size)]
     for partner in partners:
@@ -210,6 +224,22 @@
 
     def list_copy(source, to, send_sem, recv_sem, k):
         return remote(source.at[k], to.at[k], send_sem.at[k], recv_sem.at[k], behind(me, shift_of(k)))
+
+    def far_first(field, j):
+        out, mid = ((far_p, far_p_mid), (far_w, far_w_mid))[field]
+        return [remote(out.at[j, way], mid.at[j, way], far_sem.at[field, 0, j, way], far_sem.at[field, 1, j, way],
+                       beside(me, way)) for way in range(2)]
+
+    def far_second(field, j):
+        mid, to = ((far_p_mid, far_p_in), (far_w_mid, far_w_in))[field]
+        return [remote(mid.at[j, way], to.at[j, way], far_sem.at[field, 2, j, way], far_sem.at[field, 3, j, way],
+                       behind(beside(me, 1 - way), SHIFTS[FAR[j]])) for way in range(2)]
+
+    def pass_on(field):
+        for j in range(len(FAR)):
+            for first_leg, second_leg in zip(far_first(field, j), far_second(field, j)):
+                first_leg.wait()
+                second_leg.start()
 
     def transpose_primal(step, carry):
         to_cell_major(p_t, 0, primal, step)
@@ -234,6 +264,13 @@
     for copy in edges:
         copy.start()
 
+    for j, k in enumerate(FAR):
+        gather_list(picked, p_t, send, k)
+        to_cell_major(padded, CHILD, dual, j)
+        pack_halves(far_p, j, picked)
+        for copy in far_first(0, j):
+            copy.start()
+
     def send_primal(step, carry):
         k = lax.rem(step + FIRST_LIST, NEIGH)
         gather_list(picked, p_t, send, k)
@@ -242,7 +279,8 @@
         list_copy(p_out, p_in, p_send, p_recv, k).start()
         return carry
 
-    lax.fori_loop(0, NEIGH, send_primal, 0)
+    lax.fori_loop(len(FAR), NEIGH, send_primal, 0)
+    pass_on(0)
     padded[CELLS + 8 :, :] = jnp.zeros((padded.shape[0] - CELLS - 8, LANES), F32)
 
     def split_recon(step, carry):
@@ -283,36 +321,56 @@
     padded[0:8, :] = before[...]
     rebuild(head, live, padded, after, after2, recon3, families, rebuilt, woven)
 
+    def local_part(step):
+        at = pl.multiple_of(step * 256, 256)
+        fill_table(table, at, p_t[pl.ds(at, 256), :], woven[pl.ds(CHILD - head + at, 256), :], operator3)
+        cell_terms(term, load, woven, CHILD - head, cell_size, step)
+
+    for j, k in enumerate(FAR):
+        gather_rows(picked, 0, woven, lambda i: send[k, i] + (CHILD - head), GHOST)
+        pack_halves(far_w, j, picked)
+        for copy in far_first(1, j):
+            copy.start()
+        local_part(jnp.int32(j))
+
     def send_weight(step, carry):
         k = lax.rem(step + FIRST_LIST, NEIGH)
-        at = pl.multiple_of(step * 256, 256)
         gather_rows(picked, 0, woven, lambda i: send[k, i] + (CHILD - head), GHOST)
-        fill_table(table, at, p_t[pl.ds(at, 256), :], woven[pl.ds(CHILD - head + at, 256), :], operator3)
-        cell_terms(term, load, woven, CHILD - head, cell_size, step)
+        local_part(step)
         pack(w_out.at[k], picked)
         list_copy(w_out, w_in, w_send, w_recv, k).start()
         return carry
 
-    lax.fori_loop(0, NEIGH, send_weight, 0)
+    lax.fori_loop(len(FAR), NEIGH, send_weight, 0)
+    pass_on(1)
     copy_a.wait()
     copy_b.wait()
 
-    def take_ghosts(step, carry):
-        k = lax.rem(step + FIRST_LIST, NEIGH)
-        list_copy(p_out, p_in, p_send, p_recv, k).wait()
-        list_copy(w_out, w_in, w_send, w_recv, k).wait()
+    def take_list(step, k, p_rows, w_rows):
         row = step * 6
         gather_rows(side_a, row * LANES, table, lambda i: smem_a[row + i // LANES, i % LANES], 256)
-        fill_table(table, CELLS + k * GHOST, unpack(p_in[k]), unpack(w_in[k]), operator3)
+        fill_table(table, CELLS + k * GHOST, unpack(p_rows), unpack(w_rows), operator3)
 
         def rest(r, carry):
             gather_rows(side_a, r * LANES, table, lambda i: smem_a[r, i], LANES)
             return carry
 
         lax.fori_loop(row + 2, row + 6, rest, 0)
+
+    def take_ghosts(step, carry):
+        k = lax.rem(step + FIRST_LIST + len(FAR), NEIGH)
+        list_copy(p_out, p_in, p_send, p_recv, k).wait()
+        list_copy(w_out, w_in, w_send, w_recv, k).wait()
+        take_list(step, k, p_in[k], w_in[k])
         return carry
 
-    lax.fori_loop(0, NEIGH, take_ghosts, 0)
+    lax.fori_loop(0, NEIGH - len(FAR), take_ghosts, 0)
+    for j, k in enumerate(FAR):
+        for field in range(2):
+            for copy in far_second(field, j):
+                copy.wait()
+        take_list(jnp.int32(NEIGH - len(FAR) + j), k, jnp.concatenate([far_p_in[j, 0], far_p_in[j, 1]], 0),
+                  jnp.concatenate([far_w_in[j, 0], far_w_in[j, 1]], 0))
 
     lane = lax.broadcasted_iota(I32, (8, 2 * LANES), 1) % LANES
     sub = lax.broadcasted_iota(I32, (8, 2 * LANES), 0)
@@ -414,6 +472,7 @@
         f32(CELLS, LANES),
         f32(8, LANES), f32(8, LANES), f32(8, LANES), f32(8, LANES), f32(16, LANES),
         f32(NEIGH, PACKED, LANES), f32(NEIGH, PACKED, LANES), f32(NEIGH, PACKED, LANES), f32(NEIGH, PACKED, LANES),
+        *[f32(len(FAR), 2, THIRD, LANES)] * 6, pltpu.SemaphoreType.DMA((2, 4, len(FAR), 2)),
         f32(3 * THIRD, LANES),
         f32(FAMILIES * CHILD + 8, LANES), f32(FAMILIES * CHILD, LANES), f32(FAMILIES, 768), f32(FAMILIES, 768),
         f32(384, 256), bf16(768, 384), f32(3 * SLOTS, LANES), f32(FACES, LANES), f32(CHUNK, LANES), f32(CHUNK, LANES),

time: 56.8 us -> 62.1 us (1.093)
  Pallas kernels: 54.6 us -> 59.9 us
    pallas_call x1, Pallas kernels: 54.6 us -> 59.9 us  [per_device(): pl.pallas_call(kernel, out_shape=[jax.ShapeDtypeStruct((cells, LANES), F3...]
where the time goes in v10:
time: 62.1 us; the launch traced here: 61.9 us
  Pallas kernels  59.9 us (96%)
  other arithmetic  1.32 us (2%)
  between operations  0.64 us (1%)
    pallas_call x1, Pallas kernels, per_device(): pl.pallas_call(kernel, out_shape=[jax.ShapeDtypeStruct((cells, LANES), F3...  59.9 us
    div x1, other arithmetic, per_device(): return (indicator, jnp.abs(indicator) / (jnp.abs(facts) + 1e-06))  1.32 us

profile of v10, /device:TPU:0, one launch (start us, length us, event | category | flops | bytes accessed | tf_op | source)
XLA Modules:
  0.0 61.9 jit_solution(16192092651993161646)
XLA Ops:
  0.6 59.9 %indicators.1 = (f32[16,128]{1,0:T(8,128)}, f32[16,128]{1,0:T(8,128)}) custom-call(s32[128]{0:T(128)} %counts.1, s32[8,256]{1,0:T(8,128)} %bitcast.11, f32[81,2048]{1,0:T(8,128)} %primal_in.1, f32[81,2048]{1,0:T(8,128)} %dual_in.1, f32[81,2048]{1,0:T(8,128)} %load_in.1, f32[16,128]{1,0:T(8,128)} %bitcast.17, s32[8,256]{1,0:T(8,128)} %bitcast.12, ...), custom_call_target="tpu_custom_call" | custom-call | tf_op jit(solution)/shard_map/indicators/pallas_call | solution.py:485
  60.6 1.3 %bitcast_divide_fusion = (f32[2048]{0:T(1024)}, f32[2048]{0:T(1024)}) fusion(f32[16,128]{1,0:T(8,128)} %get-tuple-element.4, f32[16,128]{1,0:T(8,128)} %get-tuple-element.5), kind=kLoop, calls=%fused_computation | loop fusion | flops 12288 | bytes 32768 | tf_op jit(solution)/shard_map/div | solution.py:496

commit v11 on v9

--- a/solution.py
+++ b/solution.py
@@ -126,6 +126,8 @@
 RANKS = 128
 SHIFTS = [(1 << which // 2) * (1 - 2 * (which % 2)) for which in range(NEIGH)]
 FIRST_LIST = 4
+LATE = 2
+EARLY = FACES // LANES - NEIGH * LATE
 SEND_ORDER = [4, 5, 6, 7, 2, 3, 0, 1]
 STAGES = ((1, 8), (8, 16))
 
@@ -297,21 +299,20 @@
     copy_a.wait()
     copy_b.wait()
 
+    def gather_a(r, carry):
+        gather_rows(side_a, r * LANES, table, lambda i: smem_a[r, i], LANES)
+        return carry
+
     def take_ghosts(step, carry):
         k = lax.rem(step + FIRST_LIST, NEIGH)
         list_copy(p_out, p_in, p_send, p_recv, k).wait()
         list_copy(w_out, w_in, w_send, w_recv, k).wait()
-        row = step * 6
-        gather_rows(side_a, row * LANES, table, lambda i: smem_a[row + i // LANES, i % LANES], 256)
+        row = EARLY + step * LATE
+        gather_rows(side_a, row * LANES, table, lambda i: smem_a[row + i // LANES, i % LANES], LATE * LANES)
         fill_table(table, CELLS + k * GHOST, unpack(p_in[k]), unpack(w_in[k]), operator3)
-
-        def rest(r, carry):
-            gather_rows(side_a, r * LANES, table, lambda i: smem_a[r, i], LANES)
-            return carry
-
-        lax.fori_loop(row + 2, row + 6, rest, 0)
-        return carry
-
+        return carry
+
+    lax.fori_loop(0, EARLY, gather_a, 0)
     lax.fori_loop(0, NEIGH, take_ghosts, 0)
 
     lane = lax.broadcasted_iota(I32, (8, 2 * LANES), 1) % LANES

time: 56.8 us -> 55.9 us (0.984)
  Pallas kernels: 54.6 us -> 53.7 us
    pallas_call x1, Pallas kernels: 54.6 us -> 53.7 us  [per_device(): pl.pallas_call(kernel, out_shape=[jax.ShapeDtypeStruct((cells, LANES), F3...]
where the time goes in v11:
time: 55.9 us; the launch traced here: 55.7 us
  Pallas kernels  53.7 us (96%)
  other arithmetic  1.32 us (2%)
  between operations  0.64 us (1%)
    pallas_call x1, Pallas kernels, per_device(): pl.pallas_call(kernel, out_shape=[jax.ShapeDtypeStruct((cells, LANES), F3...  53.7 us
    div x1, other arithmetic, per_device(): return (indicator, jnp.abs(indicator) / (jnp.abs(facts) + 1e-06))  1.32 us

profile of v11, /device:TPU:0, one launch (start us, length us, event | category | flops | bytes accessed | tf_op | source)
XLA Modules:
  0.0 55.7 jit_solution(3604315777111864570)
XLA Ops:
  0.6 53.7 %indicators.1 = (f32[16,128]{1,0:T(8,128)}, f32[16,128]{1,0:T(8,128)}) custom-call(s32[128]{0:T(128)} %counts.1, s32[8,256]{1,0:T(8,128)} %bitcast.11, f32[81,2048]{1,0:T(8,128)} %primal_in.1, f32[81,2048]{1,0:T(8,128)} %dual_in.1, f32[81,2048]{1,0:T(8,128)} %load_in.1, f32[16,128]{1,0:T(8,128)} %bitcast.17, s32[8,256]{1,0:T(8,128)} %bitcast.12, ...), custom_call_target="tpu_custom_call" | custom-call | tf_op jit(solution)/shard_map/indicators/pallas_call | solution.py:427
  54.4 1.3 %bitcast_divide_fusion = (f32[2048]{0:T(1024)}, f32[2048]{0:T(1024)}) fusion(f32[16,128]{1,0:T(8,128)} %get-tuple-element.4, f32[16,128]{1,0:T(8,128)} %get-tuple-element.5), kind=kLoop, calls=%fused_computation | loop fusion | flops 12288 | bytes 32768 | tf_op jit(solution)/shard_map/div | solution.py:438

commit v12 on v11

--- a/solution.py
+++ b/solution.py
@@ -287,15 +287,19 @@
 
     def send_weight(step, carry):
         k = lax.rem(step + FIRST_LIST, NEIGH)
+        gather_rows(picked, 0, woven, lambda i: send[k, i] + (CHILD - head), GHOST)
+        pack(w_out.at[k], picked)
+        list_copy(w_out, w_in, w_send, w_recv, k).start()
+        return carry
+
+    def local_part(step, carry):
         at = pl.multiple_of(step * 256, 256)
-        gather_rows(picked, 0, woven, lambda i: send[k, i] + (CHILD - head), GHOST)
         fill_table(table, at, p_t[pl.ds(at, 256), :], woven[pl.ds(CHILD - head + at, 256), :], operator3)
         cell_terms(term, load, woven, CHILD - head, cell_size, step)
-        pack(w_out.at[k], picked)
-        list_copy(w_out, w_in, w_send, w_recv, k).start()
         return carry
 
     lax.fori_loop(0, NEIGH, send_weight, 0)
+    lax.fori_loop(0, NEIGH, local_part, 0)
     copy_a.wait()
     copy_b.wait()
 

time: 55.9 us -> 57.5 us (1.029)
  Pallas kernels: 53.7 us -> 55.4 us
    pallas_call x1, Pallas kernels: 53.7 us -> 55.4 us  [per_device(): pl.pallas_call(kernel, out_shape=[jax.ShapeDtypeStruct((cells, LANES), F3...]
where the time goes in v12:
time: 57.5 us; the launch traced here: 57.3 us
  Pallas kernels  55.4 us (96%)
  other arithmetic  1.32 us (2%)
  between operations  0.64 us (1%)
    pallas_call x1, Pallas kernels, per_device(): pl.pallas_call(kernel, out_shape=[jax.ShapeDtypeStruct((cells, LANES), F3...  55.4 us
    div x1, other arithmetic, per_device(): return (indicator, jnp.abs(indicator) / (jnp.abs(facts) + 1e-06))  1.32 us

profile of v12, /device:TPU:0, one launch (start us, length us, event | category | flops | bytes accessed | tf_op | source)
XLA Modules:
  0.0 57.3 jit_solution(5920968132139794215)
XLA Ops:
  0.6 55.4 %indicators.1 = (f32[16,128]{1,0:T(8,128)}, f32[16,128]{1,0:T(8,128)}) custom-call(s32[128]{0:T(128)} %counts.1, s32[8,256]{1,0:T(8,128)} %bitcast.11, f32[81,2048]{1,0:T(8,128)} %primal_in.1, f32[81,2048]{1,0:T(8,128)} %dual_in.1, f32[81,2048]{1,0:T(8,128)} %load_in.1, f32[16,128]{1,0:T(8,128)} %bitcast.17, s32[8,256]{1,0:T(8,128)} %bitcast.12, ...), custom_call_target="tpu_custom_call" | custom-call | tf_op jit(solution)/shard_map/indicators/pallas_call | solution.py:431
  56.0 1.3 %bitcast_divide_fusion = (f32[2048]{0:T(1024)}, f32[2048]{0:T(1024)}) fusion(f32[16,128]{1,0:T(8,128)} %get-tuple-element.4, f32[16,128]{1,0:T(8,128)} %get-tuple-element.5), kind=kLoop, calls=%fused_computation | loop fusion | flops 12288 | bytes 32768 | tf_op jit(solution)/shard_map/div | solution.py:442

commit v13 on v11

--- a/solution.py
+++ b/solution.py
@@ -236,30 +236,28 @@
     for copy in edges:
         copy.start()
 
+    for i in range(2, len(staged)):
+        loads[i].wait()
+
     def send_primal(step, carry):
         k = lax.rem(step + FIRST_LIST, NEIGH)
         gather_list(picked, p_t, send, k)
         to_cell_major(padded, CHILD, dual, step)
-        pack(p_out.at[k], picked)
-        list_copy(p_out, p_in, p_send, p_recv, k).start()
-        return carry
-
-    lax.fori_loop(0, NEIGH, send_primal, 0)
-    padded[CELLS + 8 :, :] = jnp.zeros((padded.shape[0] - CELLS - 8, LANES), F32)
-
-    def split_recon(step, carry):
+        take_residual(load, primal, stiffness, step)
+        onehot[:, pl.ds(pl.multiple_of(step * GHOST, GHOST), GHOST)] = low_onehot(send_v[pl.ds(step, 1), :])
         rows = pl.ds(pl.multiple_of(step * 96, 96), 96)
         wide = jnp.concatenate([recon[rows, :], jnp.zeros((96, 768 - CHILD * DOF), F32)], 1)
         hi, lo = split(wide)
         recon3[rows, 0:768] = hi
         recon3[rows, 768:1536] = hi
         recon3[rows, 1536:2304] = lo
+        pack(p_out.at[k], picked)
+        list_copy(p_out, p_in, p_send, p_recv, k).start()
         return carry
 
-    loads[2].wait()
-    lax.fori_loop(0, 7, split_recon, 0)
-    for i in range(3, len(staged)):
-        loads[i].wait()
+    lax.fori_loop(0, NEIGH, send_primal, 0)
+    padded[CELLS + 8 :, :] = jnp.zeros((padded.shape[0] - CELLS - 8, LANES), F32)
+
     fill_operator(operator, traction, trace)
     hi, lo = split(operator[...].T)
     operator3[0:256, :] = hi
@@ -273,13 +271,6 @@
     copy_a.start()
     copy_b.start()
 
-    def residuals(step, carry):
-        take_residual(load, primal, stiffness, step)
-        return carry
-
-    lax.fori_loop(0, 8, residuals, 0)
-    for k in range(NEIGH):
-        onehot[:, k * GHOST : (k + 1) * GHOST] = low_onehot(send_v[k : k + 1, :])
     for copy in edges:
         copy.wait()
     padded[0:8, :] = before[...]

time: 55.9 us -> 54.8 us (0.980)
  Pallas kernels: 53.7 us -> 52.7 us
    pallas_call x1, Pallas kernels: 53.7 us -> 52.7 us  [per_device(): pl.pallas_call(kernel, out_shape=[jax.ShapeDtypeStruct((cells, LANES), F3...]
where the time goes in v13:
time: 54.8 us; the launch traced here: 54.6 us
  Pallas kernels  52.7 us (96%)
  other arithmetic  1.32 us (2%)
  between operations  0.64 us (1%)
    pallas_call x1, Pallas kernels, per_device(): pl.pallas_call(kernel, out_shape=[jax.ShapeDtypeStruct((cells, LANES), F3...  52.7 us
    div x1, other arithmetic, per_device(): return (indicator, jnp.abs(indicator) / (jnp.abs(facts) + 1e-06))  1.32 us

profile of v13, /device:TPU:0, one launch (start us, length us, event | category | flops | bytes accessed | tf_op | source)
XLA Modules:
  0.0 54.6 jit_solution(10919233584023126316)
XLA Ops:
  0.6 52.7 %indicators.1 = (f32[16,128]{1,0:T(8,128)}, f32[16,128]{1,0:T(8,128)}) custom-call(s32[128]{0:T(128)} %counts.1, s32[8,256]{1,0:T(8,128)} %bitcast.11, f32[81,2048]{1,0:T(8,128)} %primal_in.1, f32[81,2048]{1,0:T(8,128)} %dual_in.1, f32[81,2048]{1,0:T(8,128)} %load_in.1, f32[16,128]{1,0:T(8,128)} %bitcast.17, s32[8,256]{1,0:T(8,128)} %bitcast.12, ...), custom_call_target="tpu_custom_call" | custom-call | tf_op jit(solution)/shard_map/indicators/pallas_call | solution.py:418
  53.3 1.3 %bitcast_divide_fusion = (f32[2048]{0:T(1024)}, f32[2048]{0:T(1024)}) fusion(f32[16,128]{1,0:T(8,128)} %get-tuple-element.4, f32[16,128]{1,0:T(8,128)} %get-tuple-element.5), kind=kLoop, calls=%fused_computation | loop fusion | flops 12288 | bytes 32768 | tf_op jit(solution)/shard_map/div | solution.py:429

commit v14 on v13

--- a/solution.py
+++ b/solution.py
@@ -90,6 +90,7 @@
     out = dot_nn(jnp.concatenate([hi, lo, hi], 1), operator[...])
     for pair in range(3):
         table[pl.ds(pl.multiple_of(pair * SLOTS + slot, 256), 256), :] = out[:, pair * LANES : (pair + 1) * LANES]
+    return hi[:, LANES:], lo[:, LANES:]
 
 
 def take_residual(load, primal, stiffness, step):
@@ -99,12 +100,17 @@
     load[:, cells] = load[:, cells] - (dot_nn(s_hi, p_hi) + dot_nn(s_lo, p_hi) + dot_nn(s_hi, p_lo))
 
 
-def cell_terms(out, residual, woven, skip, cell_size, step):
-    cells = pl.ds(pl.multiple_of(step * 256, 256), 256)
-    total = jnp.sum(residual[:, cells] * woven[pl.ds(skip + step * 256, 256), :].T[:DOF, :], axis=0, keepdims=True)
+def cell_terms(out, residual, w_hi, w_lo, cell_size, step):
+    r_hi, r_lo = split(residual[:, pl.ds(pl.multiple_of(step * 256, 256), 256)])
+    square = (LANES, LANES)
+    same = lax.broadcasted_iota(I32, square, 0) == lax.broadcasted_iota(I32, square, 1)
     for r in range(2):
+        part = slice(r * LANES, (r + 1) * LANES)
+        w_h, w_l, r_h, r_l = w_hi[part, :DOF], w_lo[part, :DOF], r_hi[:, part], r_lo[:, part]
+        pairs = dot_nn(w_h, r_h) + dot_nn(w_l, r_h) + dot_nn(w_h, r_l)
+        total = jnp.sum(jnp.where(same, pairs, 0.0), axis=0, keepdims=True)
         i = step * 2 + r
-        out[pl.ds(i, 1), :] = cell_size[pl.ds(i, 1), :] * total[:, r * LANES : (r + 1) * LANES]
+        out[pl.ds(i, 1), :] = cell_size[pl.ds(i, 1), :] * total
 
 
 def lanes_of(ref, chunk):
@@ -213,13 +219,10 @@
     def list_copy(source, to, send_sem, recv_sem, k):
         return remote(source.at[k], to.at[k], send_sem.at[k], recv_sem.at[k], behind(me, shift_of(k)))
 
-    def transpose_primal(step, carry):
+    loads[0].wait()
+    loads[1].wait()
+    for step in range(8):
         to_cell_major(p_t, 0, primal, step)
-        return carry
-
-    loads[0].wait()
-    lax.fori_loop(0, 8, transpose_primal, 0)
-    loads[1].wait()
     cell = lax.broadcasted_iota(I32, (16, CELLS), 1)
     row = lax.broadcasted_iota(I32, (16, CELLS), 0)
     picked_cell = jnp.where(row < CHILD, row, live - 2 * CHILD + row)
@@ -280,8 +283,8 @@
         k = lax.rem(step + FIRST_LIST, NEIGH)
         at = pl.multiple_of(step * 256, 256)
         gather_rows(picked, 0, woven, lambda i: send[k, i] + (CHILD - head), GHOST)
-        fill_table(table, at, p_t[pl.ds(at, 256), :], woven[pl.ds(CHILD - head + at, 256), :], operator3)
-        cell_terms(term, load, woven, CHILD - head, cell_size, step)
+        w_hi, w_lo = fill_table(table, at, p_t[pl.ds(at, 256), :], woven[pl.ds(CHILD - head + at, 256), :], operator3)
+        cell_terms(term, load, w_hi, w_lo, cell_size, step)
         pack(w_out.at[k], picked)
         list_copy(w_out, w_in, w_send, w_recv, k).start()
         return carry

time: 54.8 us -> 54.8 us (level)
  no operation moved by 1% of the time
where the time goes in v14:
time: 54.8 us; the launch traced here: 54.6 us
  Pallas kernels  52.6 us (96%)
  other arithmetic  1.32 us (2%)
  between operations  0.64 us (1%)
    pallas_call x1, Pallas kernels, per_device(): pl.pallas_call(kernel, out_shape=[jax.ShapeDtypeStruct((cells, LANES), F3...  52.6 us
    div x1, other arithmetic, per_device(): return (indicator, jnp.abs(indicator) / (jnp.abs(facts) + 1e-06))  1.32 us

profile of v14, /device:TPU:0, one launch (start us, length us, event | category | flops | bytes accessed | tf_op | source)
XLA Modules:
  0.0 54.6 jit_solution(10045225744456695408)
XLA Ops:
  0.6 52.6 %indicators.1 = (f32[16,128]{1,0:T(8,128)}, f32[16,128]{1,0:T(8,128)}) custom-call(s32[128]{0:T(128)} %counts.1, s32[8,256]{1,0:T(8,128)} %bitcast.11, f32[81,2048]{1,0:T(8,128)} %primal_in.1, f32[81,2048]{1,0:T(8,128)} %dual_in.1, f32[81,2048]{1,0:T(8,128)} %load_in.1, f32[16,128]{1,0:T(8,128)} %bitcast.17, s32[8,256]{1,0:T(8,128)} %bitcast.12, ...), custom_call_target="tpu_custom_call" | custom-call | tf_op jit(solution)/shard_map/indicators/pallas_call | solution.py:421
  53.3 1.3 %bitcast_divide_fusion = (f32[2048]{0:T(1024)}, f32[2048]{0:T(1024)}) fusion(f32[16,128]{1,0:T(8,128)} %get-tuple-element.4, f32[16,128]{1,0:T(8,128)} %get-tuple-element.5), kind=kLoop, calls=%fused_computation | loop fusion | flops 12288 | bytes 32768 | tf_op jit(solution)/shard_map/div | solution.py:432

commit v15 on v13

--- a/solution.py
+++ b/solution.py
@@ -126,7 +126,7 @@
 RANKS = 128
 SHIFTS = [(1 << which // 2) * (1 - 2 * (which % 2)) for which in range(NEIGH)]
 FIRST_LIST = 4
-LATE = 2
+LATE = 3
 EARLY = FACES // LANES - NEIGH * LATE
 SEND_ORDER = [4, 5, 6, 7, 2, 3, 0, 1]
 STAGES = ((1, 8), (8, 16))

time: 54.8 us -> 54.4 us (level)
  no operation moved by 1% of the time
where the time goes in v15:
time: 54.4 us; the launch traced here: 54.2 us
  Pallas kernels  52.2 us (96%)
  other arithmetic  1.32 us (2%)
  between operations  0.64 us (1%)
    pallas_call x1, Pallas kernels, per_device(): pl.pallas_call(kernel, out_shape=[jax.ShapeDtypeStruct((cells, LANES), F3...  52.2 us
    div x1, other arithmetic, per_device(): return (indicator, jnp.abs(indicator) / (jnp.abs(facts) + 1e-06))  1.32 us

profile of v15, /device:TPU:0, one launch (start us, length us, event | category | flops | bytes accessed | tf_op | source)
XLA Modules:
  0.0 54.2 jit_solution(2636578370124262204)
XLA Ops:
  0.6 52.2 %indicators.1 = (f32[16,128]{1,0:T(8,128)}, f32[16,128]{1,0:T(8,128)}) custom-call(s32[128]{0:T(128)} %counts.1, s32[8,256]{1,0:T(8,128)} %bitcast.11, f32[81,2048]{1,0:T(8,128)} %primal_in.1, f32[81,2048]{1,0:T(8,128)} %dual_in.1, f32[81,2048]{1,0:T(8,128)} %load_in.1, f32[16,128]{1,0:T(8,128)} %bitcast.17, s32[8,256]{1,0:T(8,128)} %bitcast.12, ...), custom_call_target="tpu_custom_call" | custom-call | tf_op jit(solution)/shard_map/indicators/pallas_call | solution.py:418
  52.9 1.3 %bitcast_divide_fusion = (f32[2048]{0:T(1024)}, f32[2048]{0:T(1024)}) fusion(f32[16,128]{1,0:T(8,128)} %get-tuple-element.4, f32[16,128]{1,0:T(8,128)} %get-tuple-element.5), kind=kLoop, calls=%fused_computation | loop fusion | flops 12288 | bytes 32768 | tf_op jit(solution)/shard_map/div | solution.py:429
